TPU v7x, 32 devices: a whole 2x2x4 slice. The times are simulated.
32 devices in a mesh: freq: 4 (over y, x), row: 4 (over z), col: 2 (over core).
Axes of the slice: x: 2, y: 2, z: 4, core: 2. Of those that a mesh axis runs over, the one named last changes fastest.
Arguments:
- pair_block: bfloat16 [192, 8192], P('freq', 'row'), may hold values from -6 to 6
- screened: bfloat16 [16, 8192, 8192], P('freq', 'row', 'col'), may hold values from -0.0625 to 0.0625
- pair_gaps: float32 [192], replicated, may hold values from 0.5 to 4
- omega_values: float32 [16], replicated, may hold values from 0.25 to 8
- quad_weight: float32 [16], replicated, may hold values from 0.2 to 1
- freq_slot: int32 [16], replicated, may hold values from 0 to 15, each once
- block_list: int32 [16], replicated, may hold values from 0 to 15, each once
Outputs:
- gamma: float32 [192, 8192], P(('freq', 'row'), 'col')
Inputs may be any that keep to these rules, and one draw needn't show every extreme that they name: `freq_slot`: a permutation of the frequencies. `block_list`: a permutation of the blocks.
All inputs are finite; a program needn't handle non-finite values.
Results may differ from a plain program's by a relative error of at most 0.0003.
Values may be sent and summed in bfloat16 or wider, within the bound.
No kernel may reach another device: no remote copies, remote signals or barrier semaphores. Data moves between devices by JAX's collectives and lax.ppermute only.
A program may use at most 128 MiB of HBM per device.

v0:
```python
import jax
import jax.numpy as jnp
from jax import lax
from jax.sharding import PartitionSpec as P


def local(pair_block, screened, pair_gaps, omega_values, quad_weight, freq_slot, block_list):
    blocks_all = block_list.shape[0]
    rows_each = pair_gaps.shape[0] // blocks_all
    matches = block_list[:, None] == jnp.arange(blocks_all, dtype=jnp.int32)[None, :]
    gap_table = pair_gaps.reshape(blocks_all, rows_each)
    gap_rows = jnp.sum(jnp.where(matches[:, :, None], gap_table[None, :, :], 0.0), axis=1).reshape(
        -1
    )
    slots_all = freq_slot.shape[0]
    slot_match = freq_slot[:, None] == jnp.arange(slots_all, dtype=jnp.int32)[None, :]
    omega_slot = jnp.sum(jnp.where(slot_match, omega_values[None, :], 0.0), axis=1)
    weight_slot = jnp.sum(jnp.where(slot_match, quad_weight[None, :], 0.0), axis=1)
    freq_dev = screened.shape[0]
    first_slot = lax.axis_index("freq") * freq_dev
    omega_mine = lax.dynamic_slice_in_dim(omega_slot, first_slot, freq_dev)
    weight_mine = lax.dynamic_slice_in_dim(weight_slot, first_slot, freq_dev)
    factor = (
        weight_mine[:, None]
        * 2.0
        * gap_rows[None, :]
        / (gap_rows[None, :] ** 2 + omega_mine[:, None] ** 2)
    )
    gathered = lax.all_gather(pair_block, "freq", axis=0, tiled=True)
    row_groups = lax.axis_size("row")
    columns_here = screened.shape[2]
    running = jnp.zeros(
        (lax.axis_size("freq") * (rows_each * row_groups), columns_here), jnp.float32
    )
    for member in range(freq_dev):
        product = jnp.dot(gathered, screened[member], preferred_element_type=jnp.float32)
        running = running + factor[member][:, None] * product
    halfway = lax.psum_scatter(running, "freq", scatter_dimension=0, tiled=True)
    result = lax.psum_scatter(halfway, "row", scatter_dimension=0, tiled=True)
    return result


def solution(mesh):
    placed = (P("freq", "row"), P("freq", "row", "col"), P(), P(), P(), P(), P())
    return jax.shard_map(
        local, mesh=mesh, in_specs=placed, out_specs=P(("freq", "row"), "col"), check_vma=False
    )
```

profile of v0, /device:TPU:0, one launch (start us, length us, event | category | flops | bytes accessed | tf_op | source)
XLA Modules:
  0.0 141.3 jit_solution(1766687516149849190)
XLA Ops:
  6.5 0.0 reduce-scatter.4.cloned.1.call-start
  6.5 0.8 broadcast_in_dim.52
  7.3 0.1 copy.8
  7.4 0.7 iota_compare_fusion
  8.1 0.1 select_reduce_fusion
  8.2 0.1 copy.9
  8.3 0.1 mul.65
  8.4 0.9 select_reduce_fusion.2
  9.3 0.1 dynamic-slice_multiply_fusion
  9.4 0.1 add_divide_fusion
  9.5 13.8 %all_gather.3 = bf16[192,2048]{1,0:T(8,128)(2,1)S(1)} all-gather(bf16[48,2048]{1,0:T(8,128)(2,1)} %param.7), channel_id=1, replica_groups=mesh['freq'=4,'row'=4,'col'=2] {'freq'}, dimensions={0}, use_global_device_ids=true | all-gather | bytes 983040 | tf_op jit(solution)/shard_map/all_gather | solution.py:29
  23.3 7.6 %fusion.19 = f32[192,4096]{1,0:T(8,128)S(1)} fusion(bf16[192,2048]{1,0:T(8,128)(2,1)S(1)} %all_gather.3, bf16[4,2048,4096]{2,1,0:T(8,128)(2,1)} %param.8, f32[192]{0:T(256)S(1)} %bitcast.40), kind=kOutput, calls=%fused_computation.14 | convolution fusion | flops 3222011904 | bytes 20710144 | tf_op jit(solution)/shard_map/dot_general | solution.py:36
  30.9 7.7 %fusion.16 = f32[192,4096]{1,0:T(8,128)S(1)} fusion(f32[192,4096]{1,0:T(8,128)S(1)} %fusion.19, bf16[192,2048]{1,0:T(8,128)(2,1)S(1)} %all_gather.3, bf16[4,2048,4096]{2,1,0:T(8,128)(2,1)} %param.8, f32[192]{0:T(256)S(1)} %bitcast.39), kind=kOutput, calls=%fused_computation.13 | convolution fusion | flops 3222798336 | bytes 23855872 | tf_op jit(solution)/shard_map/dot_general | solution.py:36
  38.6 7.7 %fusion.25 = f32[192,4096]{1,0:T(8,128)S(1)} fusion(f32[192,4096]{1,0:T(8,128)S(1)} %fusion.16, bf16[192,2048]{1,0:T(8,128)(2,1)S(1)} %all_gather.3, bf16[4,2048,4096]{2,1,0:T(8,128)(2,1)} %param.8, f32[192]{0:T(256)S(1)} %bitcast.38), kind=kOutput, calls=%fused_computation.16 | convolution fusion | flops 3222798336 | bytes 23855872 | tf_op jit(solution)/shard_map/dot_general | solution.py:36
  46.3 11.1 %fusion.31 = f32[192,4096]{1,0:T(8,128)} fusion(f32[192,4096]{1,0:T(8,128)S(1)} %fusion.25, bf16[192,2048]{1,0:T(8,128)(2,1)S(1)} %all_gather.3, bf16[4,2048,4096]{2,1,0:T(8,128)(2,1)} %param.8, f32[192]{0:T(256)S(1)} %bitcast.37), kind=kOutput, calls=%fused_computation.18 | convolution fusion | flops 3222798336 | bytes 23855872 | tf_op jit(solution)/shard_map/dot_general | solution.py:36
  57.3 0.0 copy-start
  57.3 0.0 reduce-scatter.4.cloned.1.call-update
  57.4 44.4 %reduce-scatter.4.cloned.1.call-done = f32[48,4096]{1,0:T(8,128)} async-done(((f32[192,4096]{1,0:T(8,128)}), f32[48,4096]{1,0:T(8,128)}) %reduce-scatter.4.cloned.1.call-update) | async-done | bytes 786448 | tf_op jit(solution)/shard_map/reduce_scatter | solution.py:38
  101.8 25.9 %fusion = f32[16,4096]{1,0:T(8,128)S(1)} fusion(f32[48,4096]{1,0:T(8,128)} %reduce-scatter.4.cloned.1.call-done), kind=kCustom, calls=%all-reduce-scatter | all-reduce-scatter fusion | flops 262145 | bytes 1049088
  127.7 1.4 collective-permute-start
  129.1 0.0 copy-done
  129.1 0.6 dynamic-slice.4
  130.3 3.1 %collective-permute-done = f32[12,4096]{1,0:T(8,128)S(1)} collective-permute-done((f32[12,4096]{1,0:T(8,128)S(1)}, f32[12,4096]{1,0:T(8,128)S(1)}, u32[]{:S(2)}, u32[]{:S(2)}) %collective-permute-start) | collective-permute-done | bytes 196640
  133.4 0.3 concatenate
  133.7 0.7 constant_dynamic-slice_fusion
  (3 shorter events, 0.0 us)
Async XLA Ops:
  6.5 95.2 %reduce-scatter.4.cloned.1.call-start = ((), (), s32[]{:S(2)}) async-start(), calls=%async_computation.1 | async-start | bytes 3932160 | tf_op jit(solution)/shard_map/reduce_scatter | solution.py:38
  57.3 71.7 %copy-start = (u32[32]{0:T(128)S(1)}, u32[32]{0:T(128)}, u32[]{:S(2)}) copy-start(u32[32]{0:T(128)} %constant.17) | copy-start | bytes 388
  127.7 5.7 %collective-permute-start = (f32[12,4096]{1,0:T(8,128)S(1)}, f32[12,4096]{1,0:T(8,128)S(1)}, u32[]{:S(2)}, u32[]{:S(2)}) collective-permute-start(f32[12,4096]{1,0:T(8,128)S(1)} %slice.36), channel_id=1, source_target_pairs={{0,2},{2,4},{4,6},{1,3},{3,5},{5,7},{8,10},{10,12},{12,14},{9,11},... | collective-permute-start | bytes 589832
Sparse Core Ops, SparseCore 0:
  57.5 44.2 reduce-scatter.3
where the time goes:
time: 142 us; the launch traced here: 141 us
  waiting for transfers between devices  47.5 us (33%)
  blocking collectives  39.7 us (28%)
  matrix products  34 us (24%)
  between operations  14.1 us (10%)
  local copies, waits for them, and re-layouts  2.68 us (2%)
  other arithmetic  1.87 us (1%)
    reduce_scatter x1, waiting for transfers between devices, local(): halfway = lax.psum_scatter(running, 'freq', scatter_dimension=0, tiled=True)  44.4 us
    dot_general x4, matrix products, local(): jnp.dot(gathered, screened[member], preferred_element_type=jnp.float32)  34 us
    unnamed x1, blocking collectives  25.9 us
    all_gather x1, blocking collectives, local(): gathered = lax.all_gather(pair_block, 'freq', axis=0, tiled=True)  13.8 us
    unnamed x2, waiting for transfers between devices  3.08 us
  transfers between devices with their start and end apart: 2, of which 2 were waited for; matrix products, arithmetic and copies ran while one was open for 0% of the time, Pallas kernels for 0%

commit v1 on v0

v1 whole, which is shorter than its diff:
```python
import functools
import math

import jax
import jax.numpy as jnp
from jax import lax
from jax.experimental import pallas as pl
from jax.experimental.pallas import tpu as pltpu
from jax.sharding import PartitionSpec as P

LANES = 128
TOP = 32700.0
STEPS = 4.0 / math.log(2.0)
VMEM = pl.BlockSpec(memory_space=pltpu.VMEM)
ANY = pl.BlockSpec(memory_space=pl.ANY)


def peer(i, k, n):
    return i ^ k if n & (n - 1) == 0 else (i + k) % n


def send(array, axis, k, n):
    return lax.ppermute(array, axis, [(i, peer(i, k, n)) for i in range(n)])


def fetch(array, axis, k, n):
    return lax.ppermute(array, axis, [(peer(i, k, n), i) for i in range(n)])


def level(high):
    return jnp.ceil(jnp.log(jnp.maximum(high, 1e-30)) * STEPS)


def encode(x, out_ref, rows):
    width = x.shape[1]
    steps = level(jnp.max(jnp.abs(x), axis=1, keepdims=True))
    y = x * (TOP * TOP * jnp.exp(steps * (-1.0 / STEPS)))
    code = jnp.round(y * lax.rsqrt(jnp.abs(y) + 1e-20))
    out_ref[:rows, :width] = code.astype(jnp.int32).astype(jnp.int16)
    out_ref[:rows, width:] = jnp.broadcast_to(steps, (x.shape[0], LANES)).astype(jnp.int32).astype(jnp.int16)


def decode(ref, rows):
    width = ref.shape[1] - LANES
    code = ref[:, :width].astype(jnp.int32).astype(jnp.float32)
    steps = ref[:, width:].astype(jnp.int32).astype(jnp.float32)[:, :1]
    return (code * jnp.abs(code) * (jnp.exp(steps * (1.0 / STEPS)) * (1.0 / (TOP * TOP))))[:rows]


def chunk_kernel(groups, start, tn, ring, *refs):
    b_refs, (fac_ref, w_ref), rest = refs[:groups], refs[groups : groups + 2], refs[groups + 2 :]
    own_ref, msg_refs, (all_rows, acc, buf, sem) = rest[0], rest[1:groups], rest[groups:]
    members = w_ref.shape[0]
    rows, width = own_ref.shape
    pieces = members * (width // tn)
    ring = min(ring, pieces)

    def copy(i, slot):
        column = pl.multiple_of(start + lax.div(i, members) * tn, tn)
        return pltpu.make_async_copy(
            w_ref.at[lax.rem(i, members), :, pl.ds(column, tn)], buf.at[slot], sem.at[slot]
        )

    for i in range(ring):
        copy(i, i).start()
    for k in range(groups):
        all_rows[k * rows : (k + 1) * rows, :] = b_refs[k][...]

    def piece(i, carry):
        slot, member = lax.rem(i, ring), lax.rem(i, members)
        copy(i, slot).wait()
        product = jnp.dot(all_rows[...], buf[slot], preferred_element_type=jnp.float32)
        scaled = product * jnp.tile(fac_ref[member], (1, tn // LANES))
        columns = pl.ds(pl.multiple_of(lax.div(i, members) * tn, tn), tn)

        @pl.when(member == 0)
        def _():
            acc[:, columns] = scaled

        @pl.when(member > 0)
        def _():
            acc[:, columns] += scaled

        @pl.when(i + ring < pieces)
        def _():
            copy(i + ring, slot).start()

        return carry

    lax.fori_loop(0, pieces, piece, 0)
    own_ref[...] = acc[:rows, :]
    for k in range(1, groups):
        encode(acc[k * rows : (k + 1) * rows, :], msg_refs[k - 1], rows)


def chunk(blocks, factor, screened, start, width, tn):
    groups, (rows, depth) = len(blocks), blocks[0].shape
    members = screened.shape[0]
    ring = 6
    outs = [jax.ShapeDtypeStruct((rows, width), jnp.float32)]
    outs += [jax.ShapeDtypeStruct((rows, width + LANES), jnp.int16)] * (groups - 1)
    return pl.pallas_call(
        functools.partial(chunk_kernel, groups, start, tn, ring),
        in_specs=[VMEM] * (groups + 1) + [ANY],
        out_specs=[VMEM] * groups,
        out_shape=outs,
        scratch_shapes=[
            pltpu.VMEM((groups * rows, depth), jnp.bfloat16),
            pltpu.VMEM((groups * rows, width), jnp.float32),
            pltpu.VMEM((ring, depth, tn), jnp.bfloat16),
            pltpu.SemaphoreType.DMA((ring,)),
        ],
        compiler_params=pltpu.CompilerParams(vmem_limit_bytes=40 << 20),
        cost_estimate=pl.CostEstimate(
            flops=2 * groups * rows * depth * width * members,
            bytes_accessed=2 * members * depth * width,
            transcendentals=0,
        ),
        name="weighted_products",
    )(*blocks, factor, screened)


def middle_kernel(groups, members, each, *refs):
    own_ref, got_refs, (mine_ref, *out_refs), total = refs[0], refs[1:groups], refs[groups:-1], refs[-1]
    rows = own_ref.shape[0]
    x = own_ref[...]
    for ref in got_refs:
        x = x + decode(ref, rows)
    total[...] = x
    me = lax.axis_index("row")
    for target in range(members):
        for k in range(members):

            @pl.when(peer(me, k, members) == target)
            def _():
                part = total[target * each : (target + 1) * each, :]
                if k == 0:
                    mine_ref[...] = part
                else:
                    encode(part, out_refs[k - 1], each)


def middle(own, got, members):
    rows, width = own.shape
    each = rows // members
    padded = -(-each // 16) * 16
    outs = [jax.ShapeDtypeStruct((each, width), jnp.float32)]
    outs += [jax.ShapeDtypeStruct((padded, width + LANES), jnp.int16)] * (members - 1)
    return pl.pallas_call(
        functools.partial(middle_kernel, len(got) + 1, members, each),
        in_specs=[VMEM] * (len(got) + 1),
        out_specs=[VMEM] * members,
        out_shape=outs,
        scratch_shapes=[pltpu.VMEM((rows, width), jnp.float32)],
        compiler_params=pltpu.CompilerParams(vmem_limit_bytes=24 << 20),
        name="frequency_sums",
    )(own, *got)


def last_kernel(widths, members, *refs):
    out_ref = refs[-1]
    rows, start = out_ref.shape[0], 0
    for c, width in enumerate(widths):
        mine_ref, *got_refs = refs[c * members : (c + 1) * members]
        x = mine_ref[...]
        for ref in got_refs:
            x = x + decode(ref, rows)
        out_ref[:, start : start + width] = x
        start += width


def last(parts, widths, members):
    rows = parts[0].shape[0]
    return pl.pallas_call(
        functools.partial(last_kernel, widths, members),
        in_specs=[VMEM] * len(parts),
        out_specs=VMEM,
        out_shape=jax.ShapeDtypeStruct((rows, sum(widths)), jnp.float32),
        compiler_params=pltpu.CompilerParams(vmem_limit_bytes=24 << 20),
        name="row_sums",
    )(*parts)


def factors(screened, pair_gaps, omega_values, quad_weight, freq_slot, block_list, groups):
    me = lax.axis_index("freq")
    blocks_all, slots_all = block_list.shape[0], freq_slot.shape[0]
    per = blocks_all // groups
    places = jnp.concatenate([peer(me, k, groups) * per + jnp.arange(per, dtype=jnp.int32) for k in range(groups)])
    every = jnp.arange(blocks_all, dtype=jnp.int32)
    blocks = jnp.sum(jnp.where(places[:, None] == every[None, :], block_list[None, :], 0), axis=1)
    gap_table = pair_gaps.reshape(blocks_all, -1)
    gap_rows = jnp.sum(jnp.where((blocks[:, None] == every[None, :])[:, :, None], gap_table[None, :, :], 0.0), axis=1)
    gap_rows = gap_rows.reshape(-1)
    freq_dev = screened.shape[0]
    slots = lax.dynamic_slice_in_dim(freq_slot, me * freq_dev, freq_dev)
    match = slots[:, None] == jnp.arange(slots_all, dtype=jnp.int32)[None, :]
    omega = jnp.sum(jnp.where(match, omega_values[None, :], 0.0), axis=1)[:, None]
    weight = jnp.sum(jnp.where(match, quad_weight[None, :], 0.0), axis=1)[:, None]
    factor = weight * 2.0 * gap_rows[None, :] / (gap_rows[None, :] ** 2 + omega**2)
    return jnp.broadcast_to(factor[:, :, None], (*factor.shape, LANES))


def split(columns, tn):
    units = columns // tn
    shares = [units // 2, units // 4 + units // 8]
    shares = [s for s in shares if s]
    shares.append(units - sum(shares))
    return [s * tn for s in shares if s]


def local(pair_block, screened, pair_gaps, omega_values, quad_weight, freq_slot, block_list):
    groups, members = lax.axis_size("freq"), lax.axis_size("row")
    columns = screened.shape[2]
    tn = math.gcd(columns, 512)
    blocks = [pair_block] + [fetch(pair_block, "freq", k, groups) for k in range(1, groups)]
    factor = factors(screened, pair_gaps, omega_values, quad_weight, freq_slot, block_list, groups)
    widths, start, parts = split(columns, tn), 0, []
    for width in widths:
        own, *out = chunk(blocks, factor, screened, start, width, tn)
        got = [send(m, "freq", k + 1, groups) for k, m in enumerate(out)]
        mine, *out = middle(own, got, members)
        parts += [mine] + [send(m, "row", k + 1, members) for k, m in enumerate(out)]
        start += width
    return last(parts, widths, members)


def solution(mesh):
    placed = (P("freq", "row"), P("freq", "row", "col"), P(), P(), P(), P(), P())
    return jax.shard_map(
        local, mesh=mesh, in_specs=placed, out_specs=P(("freq", "row"), "col"), check_vma=False
    )
```

time: 142 us -> 78.2 us (0.55)
  blocking collectives: 39.7 us -> 0 us
  matrix products: 34 us -> 0 us
  waiting for transfers between devices: 47.5 us -> 15.7 us
  Pallas kernels: 0 us -> 29.1 us
  starting transfers between devices: 1.36 us -> 28.1 us
  between operations: 14.1 us -> 0.14 us
    reduce_scatter x1 -> x0, waiting for transfers between devices: 44.4 us -> none  [local(): halfway = lax.psum_scatter(running, 'freq', scatter_dimension=0, tiled=True)]
    dot_general x4 -> x0, matrix products: 34 us -> none  [local(): jnp.dot(gathered, screened[member], preferred_element_type=jnp.float32)]
    pallas_call x0 -> x7, Pallas kernels: none -> 29.1 us  [the longest x3 26.4 us: chunk(): pl.pallas_call(functools.partial(chunk_kernel, groups, start, tn, ring),...]
    ppermute x0 -> x21, starting transfers between devices: none -> 28.1 us  [the longest x18 23.7 us: send(): return lax.ppermute(array, axis, [(i, peer(i, k, n)) for i in range(n)])]
    unnamed x1 -> x0, blocking collectives: 25.9 us -> none
    ppermute x0 -> x21, waiting for transfers between devices: none -> 15.7 us  [the longest x18 10.3 us: send(): return lax.ppermute(array, axis, [(i, peer(i, k, n)) for i in range(n)])]
    all_gather x1 -> x0, blocking collectives: 13.8 us -> none  [local(): gathered = lax.all_gather(pair_block, 'freq', axis=0, tiled=True)]
    unnamed x2 -> x0, waiting for transfers between devices: 3.08 us -> none
  transfers between devices with their start and end apart: 2 -> 21, of which waited for: 2 -> 5; matrix products, arithmetic and copies ran while one was open for 0% -> 5% of each run, Pallas kernels for 0% -> 31%
where the time goes in v1:
time: 78.2 us; the launch traced here: 78 us
  Pallas kernels  29.1 us (37%)
  starting transfers between devices  28.1 us (36%)
  waiting for transfers between devices  15.7 us (20%)
  local copies, waits for them, and re-layouts  2.83 us (4%)
  other arithmetic  2.07 us (3%)
    pallas_call x3, Pallas kernels, chunk(): pl.pallas_call(functools.partial(chunk_kernel, groups, start, tn, ring),...  26.4 us
    ppermute x18, starting transfers between devices, send(): return lax.ppermute(array, axis, [(i, peer(i, k, n)) for i in range(n)])  23.7 us
    ppermute x18, waiting for transfers between devices, send(): return lax.ppermute(array, axis, [(i, peer(i, k, n)) for i in range(n)])  10.3 us
    ppermute x3, waiting for transfers between devices, fetch(): return lax.ppermute(array, axis, [(peer(i, k, n), i) for i in range(n)])  5.39 us
    ppermute x3, starting transfers between devices, fetch(): return lax.ppermute(array, axis, [(peer(i, k, n), i) for i in range(n)])  4.46 us
    pallas_call x3, Pallas kernels, middle(): pl.pallas_call(functools.partial(middle_kernel, len(got) + 1, members, ea...  1.88 us
  transfers between devices with their start and end apart: 21, of which 5 were waited for; matrix products, arithmetic and copies ran while one was open for 5% of the time, Pallas kernels for 31%

profile of v1, /device:TPU:0, one launch (start us, length us, event | category | flops | bytes accessed | tf_op | source)
XLA Modules:
  0.0 78.0 jit_solution(9503376628898853410)
XLA Ops:
  0.0 2.9 %collective-permute-start = (bf16[48,2048]{1,0:T(8,128)(2,1)}, bf16[48,2048]{1,0:T(8,128)(2,1)S(1)}, u32[]{:S(2)}, u32[]{:S(2)}) collective-permute-start(bf16[48,2048]{1,0:T(8,128)(2,1)} %refs_0_.5), channel_id=1, source_target_pairs={{8,0},{0,8},{24,16},{16,24},{9,1},{1,9},{25,17},{17,25},{10,2},{2,... | collective-permute-start | bytes 589832 | tf_op jit(solution)/shard_map/ppermute | solution.py:27
  2.9 1.5 %collective-permute-start.1 = (bf16[48,2048]{1,0:T(8,128)(2,1)}, bf16[48,2048]{1,0:T(8,128)(2,1)S(1)}, u32[]{:S(2)}, u32[]{:S(2)}) collective-permute-start(bf16[48,2048]{1,0:T(8,128)(2,1)} %refs_0_.5), channel_id=1, source_target_pairs={{16,0},{24,8},{0,16},{8,24},{17,1},{25,9},{1,17},{9,25},{18,2},{26... | collective-permute-start | bytes 589832 | tf_op jit(solution)/shard_map/ppermute | solution.py:27
  4.5 0.0 collective-permute-start.2
  4.5 0.1 pad_add_fusion
  4.5 0.8 %select_reduce_fusion.1 = s32[16]{0:T(128)S(1)} fusion(s32[16]{0:T(128)} %param.13, s32[16]{0:T(128)S(1)} %pad_add_fusion), kind=kLoop, calls=%fused_computation.2 | loop fusion | flops 752 | bytes 192 | tf_op jit(solution)/shard_map/reduce_sum | solution.py:190
  5.4 0.1 iota_compare_fusion
  5.5 0.8 broadcast_in_dim.75
  6.2 0.1 copy.8
  6.3 0.1 select_reduce_fusion
  6.4 0.1 copy.9
  6.5 0.1 mul.46
  6.6 0.7 dynamic_slice.3
  7.4 0.9 %select_reduce_fusion.3 = (f32[4]{0:T(128)S(1)}, f32[4]{0:T(128)S(1)}) fusion(f32[16]{0:T(128)} %param.11, s32[4]{0:T(128)S(1)} %dynamic_slice.3, f32[16]{0:T(128)} %param.10), kind=kLoop, calls=%fused_computation.6 | loop fusion | flops 312 | bytes 176 | tf_op jit(solution)/shard_map/reduce_sum | solution.py:198
  8.3 0.1 add_divide_fusion
  8.3 0.5 collective-permute-done.refs_1_
  8.9 4.8 %collective-permute-done.1.refs_2_ = bf16[48,2048]{1,0:T(8,128)(2,1)S(1)} collective-permute-done((bf16[48,2048]{1,0:T(8,128)(2,1)}, bf16[48,2048]{1,0:T(8,128)(2,1)S(1)}, u32[]{:S(2)}, u32[]{:S(2)}) %collective-permute-start.1) | collective-permute-done | bytes 196640 | tf_op jit(solution)/shard_map/ppermute | solution.py:27
  13.7 0.0 collective-permute-done.2.refs_3_
  13.7 0.2 broadcast_in_dim.79.refs_4_
  13.9 0.0 copy-start
  13.9 0.9 %copy-done = bf16[48,2048]{1,0:T(8,128)(2,1)S(1)} copy-done((bf16[48,2048]{1,0:T(8,128)(2,1)S(1)}, bf16[48,2048]{1,0:T(8,128)(2,1)}, u32[]{:S(2)}) %copy-start) | copy-done | bytes 196632
  14.8 4.4 %weighted_products.5 = (f32[48,512]{1,0:T(8,128)S(1)}, s16[48,640]{1,0:T(8,128)(2,1)S(1)}, s16[48,640]{1,0:T(8,128)(2,1)S(1)}, s16[48,640]{1,0:T(8,128)(2,1)S(1)}) custom-call(bf16[48,2048]{1,0:T(8,128)(2,1)S(1)} %copy-done, bf16[48,2048]{1,0:T(8,128)(2,1)S(1)} %collective-permute-done.refs_1_, bf16[48,2048]{1,0:T(8,128)(2,1)S(1)} %collective-permute-done.1.refs_2_, ...), custom_call_target="tpu_custom_call" | custom-call | flops 1610612736 | bytes 8388608 | tf_op jit(solution)/shard_map/weighted_products/pallas_call | solution.py:102
  19.2 1.3 %collective-permute-start.15 = (s16[48,640]{1,0:T(8,128)(2,1)S(1)}, s16[48,640]{1,0:T(8,128)(2,1)S(1)}, u32[]{:S(2)}, u32[]{:S(2)}) collective-permute-start(s16[48,640]{1,0:T(8,128)(2,1)S(1)} %get-tuple-element.46), channel_id=1, source_target_pairs={{0,8},{8,0},{16,24},{24,16},{1,9},{9,1},{17,25},{25,17},{2,10},{10... | collective-permute-start | bytes 184328 | tf_op jit(solution)/shard_map/ppermute | solution.py:23
  20.5 9.7 %weighted_products.4 = (f32[48,1536]{1,0:T(8,128)S(1)}, s16[48,1664]{1,0:T(8,128)(2,1)S(1)}, s16[48,1664]{1,0:T(8,128)(2,1)S(1)}, s16[48,1664]{1,0:T(8,128)(2,1)S(1)}) custom-call(bf16[48,2048]{1,0:T(8,128)(2,1)S(1)} %copy-done, bf16[48,2048]{1,0:T(8,128)(2,1)S(1)} %collective-permute-done.refs_1_, bf16[48,2048]{1,0:T(8,128)(2,1)S(1)} %collective-permute-done.1.refs_2_, ...), custom_call_target="tpu_custom_call" | custom-call | flops 4831838208 | bytes 25165824 | tf_op jit(solution)/shard_map/weighted_products/pallas_call | solution.py:102
  30.2 0.9 %collective-permute-start.10 = (s16[48,1664]{1,0:T(8,128)(2,1)S(1)}, s16[48,1664]{1,0:T(8,128)(2,1)S(1)}, u32[]{:S(2)}, u32[]{:S(2)}) collective-permute-start(s16[48,1664]{1,0:T(8,128)(2,1)S(1)} %get-tuple-element.39), channel_id=1, source_target_pairs={{0,16},{8,24},{16,0},{24,8},{1,17},{9,25},{17,1},{25,9},{2,18},{10... | collective-permute-start | bytes 479240 | tf_op jit(solution)/shard_map/ppermute | solution.py:23
  31.1 1.4 %collective-permute-start.11 = (s16[48,1664]{1,0:T(8,128)(2,1)S(1)}, s16[48,1664]{1,0:T(8,128)(2,1)S(1)}, u32[]{:S(2)}, u32[]{:S(2)}) collective-permute-start(s16[48,1664]{1,0:T(8,128)(2,1)S(1)} %get-tuple-element.40), channel_id=1, source_target_pairs={{0,24},{8,16},{16,8},{24,0},{1,25},{9,17},{17,9},{25,1},{2,26},{10... | collective-permute-start | bytes 479240 | tf_op jit(solution)/shard_map/ppermute | solution.py:23
  32.5 1.2 %collective-permute-start.9 = (s16[48,1664]{1,0:T(8,128)(2,1)S(1)}, s16[48,1664]{1,0:T(8,128)(2,1)S(1)}, u32[]{:S(2)}, u32[]{:S(2)}) collective-permute-start(s16[48,1664]{1,0:T(8,128)(2,1)S(1)} %get-tuple-element.38), channel_id=1, source_target_pairs={{0,8},{8,0},{16,24},{24,16},{1,9},{9,1},{17,25},{25,17},{2,10},{10... | collective-permute-start | bytes 479240 | tf_op jit(solution)/shard_map/ppermute | solution.py:23
  33.8 12.3 %weighted_products.3 = (f32[48,2048]{1,0:T(8,128)S(1)}, s16[48,2176]{1,0:T(8,128)(2,1)S(1)}, s16[48,2176]{1,0:T(8,128)(2,1)S(1)}, s16[48,2176]{1,0:T(8,128)(2,1)S(1)}) custom-call(bf16[48,2048]{1,0:T(8,128)(2,1)S(1)} %copy-done, bf16[48,2048]{1,0:T(8,128)(2,1)S(1)} %collective-permute-done.refs_1_, bf16[48,2048]{1,0:T(8,128)(2,1)S(1)} %collective-permute-done.1.refs_2_, ...), custom_call_target="tpu_custom_call" | custom-call | flops 6442450944 | bytes 33554432 | tf_op jit(solution)/shard_map/weighted_products/pallas_call | solution.py:102
  46.1 0.9 %collective-permute-start.3 = (s16[48,2176]{1,0:T(8,128)(2,1)S(1)}, s16[48,2176]{1,0:T(8,128)(2,1)S(1)}, u32[]{:S(2)}, u32[]{:S(2)}) collective-permute-start(s16[48,2176]{1,0:T(8,128)(2,1)S(1)} %get-tuple-element.30), channel_id=1, source_target_pairs={{0,8},{8,0},{16,24},{24,16},{1,9},{9,1},{17,25},{25,17},{2,10},{10... | collective-permute-start | bytes 626696 | tf_op jit(solution)/shard_map/ppermute | solution.py:23
  46.9 0.0 collective-permute-done.15.refs_1_
  46.9 1.5 %collective-permute-start.4 = (s16[48,2176]{1,0:T(8,128)(2,1)S(1)}, s16[48,2176]{1,0:T(8,128)(2,1)S(1)}, u32[]{:S(2)}, u32[]{:S(2)}) collective-permute-start(s16[48,2176]{1,0:T(8,128)(2,1)S(1)} %get-tuple-element.31), channel_id=1, source_target_pairs={{0,16},{8,24},{16,0},{24,8},{1,17},{9,25},{17,1},{25,9},{2,18},{10... | collective-permute-start | bytes 626696 | tf_op jit(solution)/shard_map/ppermute | solution.py:23
  48.5 0.0 collective-permute-done.10.refs_2_
  48.5 1.2 %collective-permute-start.5 = (s16[48,2176]{1,0:T(8,128)(2,1)S(1)}, s16[48,2176]{1,0:T(8,128)(2,1)S(1)}, u32[]{:S(2)}, u32[]{:S(2)}) collective-permute-start(s16[48,2176]{1,0:T(8,128)(2,1)S(1)} %get-tuple-element.32), channel_id=1, source_target_pairs={{0,24},{8,16},{16,8},{24,0},{1,25},{9,17},{17,9},{25,1},{2,26},{10... | collective-permute-start | bytes 626696 | tf_op jit(solution)/shard_map/ppermute | solution.py:23
  49.6 0.0 collective-permute-done.11.refs_3_
  49.6 0.8 %collective-permute-start.16 = (s16[48,640]{1,0:T(8,128)(2,1)S(1)}, s16[48,640]{1,0:T(8,128)(2,1)S(1)}, u32[]{:S(2)}, u32[]{:S(2)}) collective-permute-start(s16[48,640]{1,0:T(8,128)(2,1)S(1)} %get-tuple-element.47), channel_id=1, source_target_pairs={{0,16},{8,24},{16,0},{24,8},{1,17},{9,25},{17,1},{25,9},{2,18},{10... | collective-permute-start | bytes 184328 | tf_op jit(solution)/shard_map/ppermute | solution.py:23
  50.5 0.0 collective-permute-done.9.refs_1_
  50.5 1.4 %collective-permute-start.17 = (s16[48,640]{1,0:T(8,128)(2,1)S(1)}, s16[48,640]{1,0:T(8,128)(2,1)S(1)}, u32[]{:S(2)}, u32[]{:S(2)}) collective-permute-start(s16[48,640]{1,0:T(8,128)(2,1)S(1)} %get-tuple-element.48), channel_id=1, source_target_pairs={{0,24},{8,16},{16,8},{24,0},{1,25},{9,17},{17,9},{25,1},{2,26},{10... | collective-permute-start | bytes 184328 | tf_op jit(solution)/shard_map/ppermute | solution.py:23
  51.9 0.6 frequency_sums.4
  52.5 5.9 %collective-permute-done.16.refs_2_ = s16[48,640]{1,0:T(8,128)(2,1)S(1)} collective-permute-done((s16[48,640]{1,0:T(8,128)(2,1)S(1)}, s16[48,640]{1,0:T(8,128)(2,1)S(1)}, u32[]{:S(2)}, u32[]{:S(2)}) %collective-permute-start.16) | collective-permute-done | bytes 61472 | tf_op jit(solution)/shard_map/ppermute | solution.py:23
  58.5 1.6 %collective-permute-start.12 = (s16[16,1664]{1,0:T(8,128)(2,1)S(1)}, s16[16,1664]{1,0:T(8,128)(2,1)S(1)}, u32[]{:S(2)}, u32[]{:S(2)}) collective-permute-start(s16[16,1664]{1,0:T(8,128)(2,1)S(1)} %get-tuple-element.42), channel_id=1, source_target_pairs={{0,2},{2,0},{4,6},{6,4},{1,3},{3,1},{5,7},{7,5},{8,10},{10,8},{12,... | collective-permute-start | bytes 159752 | tf_op jit(solution)/shard_map/ppermute | solution.py:23
  60.1 0.0 collective-permute-done.17.refs_3_
  60.1 0.5 frequency_sums.5
  60.6 0.5 collective-permute-start.18
  61.1 0.0 collective-permute-done.3.refs_1_
  61.1 2.6 %collective-permute-start.19 = (s16[16,640]{1,0:T(8,128)(2,1)S(1)}, s16[16,640]{1,0:T(8,128)(2,1)S(1)}, u32[]{:S(2)}, u32[]{:S(2)}) collective-permute-start(s16[16,640]{1,0:T(8,128)(2,1)S(1)} %get-tuple-element.51), channel_id=1, source_target_pairs={{0,4},{2,6},{4,0},{6,2},{1,5},{3,7},{5,1},{7,3},{8,12},{10,14},{12... | collective-permute-start | bytes 61448 | tf_op jit(solution)/shard_map/ppermute | solution.py:23
  63.7 0.0 collective-permute-done.4.refs_2_
  63.7 1.4 %collective-permute-start.20 = (s16[16,640]{1,0:T(8,128)(2,1)S(1)}, s16[16,640]{1,0:T(8,128)(2,1)S(1)}, u32[]{:S(2)}, u32[]{:S(2)}) collective-permute-start(s16[16,640]{1,0:T(8,128)(2,1)S(1)} %get-tuple-element.52), channel_id=1, source_target_pairs={{0,6},{2,4},{4,2},{6,0},{1,7},{3,5},{5,3},{7,1},{8,14},{10,12},{12... | collective-permute-start | bytes 61448 | tf_op jit(solution)/shard_map/ppermute | solution.py:23
  65.0 0.0 collective-permute-done.5.refs_3_
  65.0 0.7 frequency_sums.3
  65.8 0.3 collective-permute-start.6
  66.1 0.0 collective-permute-done.18.refs_9_
  66.1 2.8 %collective-permute-start.7 = (s16[16,2176]{1,0:T(8,128)(2,1)S(1)}, s16[16,2176]{1,0:T(8,128)(2,1)S(1)}, u32[]{:S(2)}, u32[]{:S(2)}) collective-permute-start(s16[16,2176]{1,0:T(8,128)(2,1)S(1)} %get-tuple-element.35), channel_id=1, source_target_pairs={{0,4},{2,6},{4,0},{6,2},{1,5},{3,7},{5,1},{7,3},{8,12},{10,14},{12... | collective-permute-start | bytes 208904 | tf_op jit(solution)/shard_map/ppermute | solution.py:23
  68.9 0.0 collective-permute-done.19.refs_10_
  68.9 1.4 %collective-permute-start.8 = (s16[16,2176]{1,0:T(8,128)(2,1)S(1)}, s16[16,2176]{1,0:T(8,128)(2,1)S(1)}, u32[]{:S(2)}, u32[]{:S(2)}) collective-permute-start(s16[16,2176]{1,0:T(8,128)(2,1)S(1)} %get-tuple-element.36), channel_id=1, source_target_pairs={{0,6},{2,4},{4,2},{6,0},{1,7},{3,5},{5,3},{7,1},{8,14},{10,12},{12... | collective-permute-start | bytes 208904 | tf_op jit(solution)/shard_map/ppermute | solution.py:23
  70.2 0.0 collective-permute-done.20.refs_11_
  70.2 0.8 %collective-permute-start.13 = (s16[16,1664]{1,0:T(8,128)(2,1)S(1)}, s16[16,1664]{1,0:T(8,128)(2,1)S(1)}, u32[]{:S(2)}, u32[]{:S(2)}) collective-permute-start(s16[16,1664]{1,0:T(8,128)(2,1)S(1)} %get-tuple-element.43), channel_id=1, source_target_pairs={{0,4},{2,6},{4,0},{6,2},{1,5},{3,7},{5,1},{7,3},{8,12},{10,14},{12... | collective-permute-start | bytes 159752 | tf_op jit(solution)/shard_map/ppermute | solution.py:23
  71.0 0.0 collective-permute-done.12.refs_5_
  71.0 1.7 %collective-permute-start.14 = (s16[16,1664]{1,0:T(8,128)(2,1)S(1)}, s16[16,1664]{1,0:T(8,128)(2,1)S(1)}, u32[]{:S(2)}, u32[]{:S(2)}) collective-permute-start(s16[16,1664]{1,0:T(8,128)(2,1)S(1)} %get-tuple-element.44), channel_id=1, source_target_pairs={{0,6},{2,4},{4,2},{6,0},{1,7},{3,5},{5,3},{7,1},{8,14},{10,12},{12... | collective-permute-start | bytes 159752 | tf_op jit(solution)/shard_map/ppermute | solution.py:23
  72.8 3.3 %collective-permute-done.13.refs_6_ = s16[16,1664]{1,0:T(8,128)(2,1)S(1)} collective-permute-done((s16[16,1664]{1,0:T(8,128)(2,1)S(1)}, s16[16,1664]{1,0:T(8,128)(2,1)S(1)}, u32[]{:S(2)}, u32[]{:S(2)}) %collective-permute-start.13) | collective-permute-done | bytes 53280 | tf_op jit(solution)/shard_map/ppermute | solution.py:23
  76.1 0.9 %collective-permute-done.14.refs_7_ = s16[16,1664]{1,0:T(8,128)(2,1)S(1)} collective-permute-done((s16[16,1664]{1,0:T(8,128)(2,1)S(1)}, s16[16,1664]{1,0:T(8,128)(2,1)S(1)}, u32[]{:S(2)}, u32[]{:S(2)}) %collective-permute-start.14) | collective-permute-done | bytes 53280 | tf_op jit(solution)/shard_map/ppermute | solution.py:23
  77.1 0.0 collective-permute-done.6.refs_1_
  77.1 0.0 collective-permute-done.7.refs_2_
  77.1 0.0 collective-permute-done.8.refs_3_
  77.1 0.9 %row_sums.1 = f32[12,4096]{1,0:T(8,128)} custom-call(f32[12,2048]{1,0:T(8,128)S(1)} %get-tuple-element.33.refs_0_, s16[16,2176]{1,0:T(8,128)(2,1)S(1)} %collective-permute-done.6.refs_1_, s16[16,2176]{1,0:T(8,128)(2,1)S(1)} %collective-permute-done.7.refs_2_, s16[16,2176]{1,0:T(8,128)(2,1)S(1)} %collective-permute-done.8.refs_3_, ...), custom_call_target="tpu_custom_call" | custom-call | tf_op jit(solution)/shard_map/row_sums/pallas_call | solution.py:174
  (5 shorter events, 0.0 us)
Async XLA Ops:
  0.0 8.9 %collective-permute-start = (bf16[48,2048]{1,0:T(8,128)(2,1)}, bf16[48,2048]{1,0:T(8,128)(2,1)S(1)}, u32[]{:S(2)}, u32[]{:S(2)}) collective-permute-start(bf16[48,2048]{1,0:T(8,128)(2,1)} %refs_0_.5), channel_id=1, source_target_pairs={{8,0},{0,8},{24,16},{16,24},{9,1},{1,9},{25,17},{17,25},{10,2},{2,... | collective-permute-start | bytes 589832 | tf_op jit(solution)/shard_map/ppermute | solution.py:27
  2.9 10.8 %collective-permute-start.1 = (bf16[48,2048]{1,0:T(8,128)(2,1)}, bf16[48,2048]{1,0:T(8,128)(2,1)S(1)}, u32[]{:S(2)}, u32[]{:S(2)}) collective-permute-start(bf16[48,2048]{1,0:T(8,128)(2,1)} %refs_0_.5), channel_id=1, source_target_pairs={{16,0},{24,8},{0,16},{8,24},{17,1},{25,9},{1,17},{9,25},{18,2},{26... | collective-permute-start | bytes 589832 | tf_op jit(solution)/shard_map/ppermute | solution.py:27
  4.5 9.3 %collective-permute-start.2 = (bf16[48,2048]{1,0:T(8,128)(2,1)}, bf16[48,2048]{1,0:T(8,128)(2,1)S(1)}, u32[]{:S(2)}, u32[]{:S(2)}) collective-permute-start(bf16[48,2048]{1,0:T(8,128)(2,1)} %refs_0_.5), channel_id=1, source_target_pairs={{24,0},{16,8},{8,16},{0,24},{25,1},{17,9},{9,17},{1,25},{26,2},{18... | collective-permute-start | bytes 589832 | tf_op jit(solution)/shard_map/ppermute | solution.py:27
  13.9 0.9 %copy-start = (bf16[48,2048]{1,0:T(8,128)(2,1)S(1)}, bf16[48,2048]{1,0:T(8,128)(2,1)}, u32[]{:S(2)}) copy-start(bf16[48,2048]{1,0:T(8,128)(2,1)} %refs_0_.5) | copy-start | bytes 589828
  19.2 27.7 %collective-permute-start.15 = (s16[48,640]{1,0:T(8,128)(2,1)S(1)}, s16[48,640]{1,0:T(8,128)(2,1)S(1)}, u32[]{:S(2)}, u32[]{:S(2)}) collective-permute-start(s16[48,640]{1,0:T(8,128)(2,1)S(1)} %get-tuple-element.46), channel_id=1, source_target_pairs={{0,8},{8,0},{16,24},{24,16},{1,9},{9,1},{17,25},{25,17},{2,10},{10... | collective-permute-start | bytes 184328 | tf_op jit(solution)/shard_map/ppermute | solution.py:23
  30.2 18.2 %collective-permute-start.10 = (s16[48,1664]{1,0:T(8,128)(2,1)S(1)}, s16[48,1664]{1,0:T(8,128)(2,1)S(1)}, u32[]{:S(2)}, u32[]{:S(2)}) collective-permute-start(s16[48,1664]{1,0:T(8,128)(2,1)S(1)} %get-tuple-element.39), channel_id=1, source_target_pairs={{0,16},{8,24},{16,0},{24,8},{1,17},{9,25},{17,1},{25,9},{2,18},{10... | collective-permute-start | bytes 479240 | tf_op jit(solution)/shard_map/ppermute | solution.py:23
  31.1 18.5 %collective-permute-start.11 = (s16[48,1664]{1,0:T(8,128)(2,1)S(1)}, s16[48,1664]{1,0:T(8,128)(2,1)S(1)}, u32[]{:S(2)}, u32[]{:S(2)}) collective-permute-start(s16[48,1664]{1,0:T(8,128)(2,1)S(1)} %get-tuple-element.40), channel_id=1, source_target_pairs={{0,24},{8,16},{16,8},{24,0},{1,25},{9,17},{17,9},{25,1},{2,26},{10... | collective-permute-start | bytes 479240 | tf_op jit(solution)/shard_map/ppermute | solution.py:23
  32.5 17.9 %collective-permute-start.9 = (s16[48,1664]{1,0:T(8,128)(2,1)S(1)}, s16[48,1664]{1,0:T(8,128)(2,1)S(1)}, u32[]{:S(2)}, u32[]{:S(2)}) collective-permute-start(s16[48,1664]{1,0:T(8,128)(2,1)S(1)} %get-tuple-element.38), channel_id=1, source_target_pairs={{0,8},{8,0},{16,24},{24,16},{1,9},{9,1},{17,25},{25,17},{2,10},{10... | collective-permute-start | bytes 479240 | tf_op jit(solution)/shard_map/ppermute | solution.py:23
  46.1 15.0 %collective-permute-start.3 = (s16[48,2176]{1,0:T(8,128)(2,1)S(1)}, s16[48,2176]{1,0:T(8,128)(2,1)S(1)}, u32[]{:S(2)}, u32[]{:S(2)}) collective-permute-start(s16[48,2176]{1,0:T(8,128)(2,1)S(1)} %get-tuple-element.30), channel_id=1, source_target_pairs={{0,8},{8,0},{16,24},{24,16},{1,9},{9,1},{17,25},{25,17},{2,10},{10... | collective-permute-start | bytes 626696 | tf_op jit(solution)/shard_map/ppermute | solution.py:23
  46.9 16.7 %collective-permute-start.4 = (s16[48,2176]{1,0:T(8,128)(2,1)S(1)}, s16[48,2176]{1,0:T(8,128)(2,1)S(1)}, u32[]{:S(2)}, u32[]{:S(2)}) collective-permute-start(s16[48,2176]{1,0:T(8,128)(2,1)S(1)} %get-tuple-element.31), channel_id=1, source_target_pairs={{0,16},{8,24},{16,0},{24,8},{1,17},{9,25},{17,1},{25,9},{2,18},{10... | collective-permute-start | bytes 626696 | tf_op jit(solution)/shard_map/ppermute | solution.py:23
  48.5 16.6 %collective-permute-start.5 = (s16[48,2176]{1,0:T(8,128)(2,1)S(1)}, s16[48,2176]{1,0:T(8,128)(2,1)S(1)}, u32[]{:S(2)}, u32[]{:S(2)}) collective-permute-start(s16[48,2176]{1,0:T(8,128)(2,1)S(1)} %get-tuple-element.32), channel_id=1, source_target_pairs={{0,24},{8,16},{16,8},{24,0},{1,25},{9,17},{17,9},{25,1},{2,26},{10... | collective-permute-start | bytes 626696 | tf_op jit(solution)/shard_map/ppermute | solution.py:23
  49.6 8.8 %collective-permute-start.16 = (s16[48,640]{1,0:T(8,128)(2,1)S(1)}, s16[48,640]{1,0:T(8,128)(2,1)S(1)}, u32[]{:S(2)}, u32[]{:S(2)}) collective-permute-start(s16[48,640]{1,0:T(8,128)(2,1)S(1)} %get-tuple-element.47), channel_id=1, source_target_pairs={{0,16},{8,24},{16,0},{24,8},{1,17},{9,25},{17,1},{25,9},{2,18},{10... | collective-permute-start | bytes 184328 | tf_op jit(solution)/shard_map/ppermute | solution.py:23
  50.5 9.6 %collective-permute-start.17 = (s16[48,640]{1,0:T(8,128)(2,1)S(1)}, s16[48,640]{1,0:T(8,128)(2,1)S(1)}, u32[]{:S(2)}, u32[]{:S(2)}) collective-permute-start(s16[48,640]{1,0:T(8,128)(2,1)S(1)} %get-tuple-element.48), channel_id=1, source_target_pairs={{0,24},{8,16},{16,8},{24,0},{1,25},{9,17},{17,9},{25,1},{2,26},{10... | collective-permute-start | bytes 184328 | tf_op jit(solution)/shard_map/ppermute | solution.py:23
  58.5 12.6 %collective-permute-start.12 = (s16[16,1664]{1,0:T(8,128)(2,1)S(1)}, s16[16,1664]{1,0:T(8,128)(2,1)S(1)}, u32[]{:S(2)}, u32[]{:S(2)}) collective-permute-start(s16[16,1664]{1,0:T(8,128)(2,1)S(1)} %get-tuple-element.42), channel_id=1, source_target_pairs={{0,2},{2,0},{4,6},{6,4},{1,3},{3,1},{5,7},{7,5},{8,10},{10,8},{12,... | collective-permute-start | bytes 159752 | tf_op jit(solution)/shard_map/ppermute | solution.py:23
  60.6 5.5 %collective-permute-start.18 = (s16[16,640]{1,0:T(8,128)(2,1)S(1)}, s16[16,640]{1,0:T(8,128)(2,1)S(1)}, u32[]{:S(2)}, u32[]{:S(2)}) collective-permute-start(s16[16,640]{1,0:T(8,128)(2,1)S(1)} %get-tuple-element.50), channel_id=1, source_target_pairs={{0,2},{2,0},{4,6},{6,4},{1,3},{3,1},{5,7},{7,5},{8,10},{10,8},{12,... | collective-permute-start | bytes 61448 | tf_op jit(solution)/shard_map/ppermute | solution.py:23
  61.1 7.8 %collective-permute-start.19 = (s16[16,640]{1,0:T(8,128)(2,1)S(1)}, s16[16,640]{1,0:T(8,128)(2,1)S(1)}, u32[]{:S(2)}, u32[]{:S(2)}) collective-permute-start(s16[16,640]{1,0:T(8,128)(2,1)S(1)} %get-tuple-element.51), channel_id=1, source_target_pairs={{0,4},{2,6},{4,0},{6,2},{1,5},{3,7},{5,1},{7,3},{8,12},{10,14},{12... | collective-permute-start | bytes 61448 | tf_op jit(solution)/shard_map/ppermute | solution.py:23
  63.7 6.6 %collective-permute-start.20 = (s16[16,640]{1,0:T(8,128)(2,1)S(1)}, s16[16,640]{1,0:T(8,128)(2,1)S(1)}, u32[]{:S(2)}, u32[]{:S(2)}) collective-permute-start(s16[16,640]{1,0:T(8,128)(2,1)S(1)} %get-tuple-element.52), channel_id=1, source_target_pairs={{0,6},{2,4},{4,2},{6,0},{1,7},{3,5},{5,3},{7,1},{8,14},{10,12},{12... | collective-permute-start | bytes 61448 | tf_op jit(solution)/shard_map/ppermute | solution.py:23
  65.8 11.3 %collective-permute-start.6 = (s16[16,2176]{1,0:T(8,128)(2,1)S(1)}, s16[16,2176]{1,0:T(8,128)(2,1)S(1)}, u32[]{:S(2)}, u32[]{:S(2)}) collective-permute-start(s16[16,2176]{1,0:T(8,128)(2,1)S(1)} %get-tuple-element.34), channel_id=1, source_target_pairs={{0,2},{2,0},{4,6},{6,4},{1,3},{3,1},{5,7},{7,5},{8,10},{10,8},{12,... | collective-permute-start | bytes 208904 | tf_op jit(solution)/shard_map/ppermute | solution.py:23
  66.1 11.0 %collective-permute-start.7 = (s16[16,2176]{1,0:T(8,128)(2,1)S(1)}, s16[16,2176]{1,0:T(8,128)(2,1)S(1)}, u32[]{:S(2)}, u32[]{:S(2)}) collective-permute-start(s16[16,2176]{1,0:T(8,128)(2,1)S(1)} %get-tuple-element.35), channel_id=1, source_target_pairs={{0,4},{2,6},{4,0},{6,2},{1,5},{3,7},{5,1},{7,3},{8,12},{10,14},{12... | collective-permute-start | bytes 208904 | tf_op jit(solution)/shard_map/ppermute | solution.py:23
  68.9 8.2 %collective-permute-start.8 = (s16[16,2176]{1,0:T(8,128)(2,1)S(1)}, s16[16,2176]{1,0:T(8,128)(2,1)S(1)}, u32[]{:S(2)}, u32[]{:S(2)}) collective-permute-start(s16[16,2176]{1,0:T(8,128)(2,1)S(1)} %get-tuple-element.36), channel_id=1, source_target_pairs={{0,6},{2,4},{4,2},{6,0},{1,7},{3,5},{5,3},{7,1},{8,14},{10,12},{12... | collective-permute-start | bytes 208904 | tf_op jit(solution)/shard_map/ppermute | solution.py:23
  70.2 5.9 %collective-permute-start.13 = (s16[16,1664]{1,0:T(8,128)(2,1)S(1)}, s16[16,1664]{1,0:T(8,128)(2,1)S(1)}, u32[]{:S(2)}, u32[]{:S(2)}) collective-permute-start(s16[16,1664]{1,0:T(8,128)(2,1)S(1)} %get-tuple-element.43), channel_id=1, source_target_pairs={{0,4},{2,6},{4,0},{6,2},{1,5},{3,7},{5,1},{7,3},{8,12},{10,14},{12... | collective-permute-start | bytes 159752 | tf_op jit(solution)/shard_map/ppermute | solution.py:23
  71.0 6.0 %collective-permute-start.14 = (s16[16,1664]{1,0:T(8,128)(2,1)S(1)}, s16[16,1664]{1,0:T(8,128)(2,1)S(1)}, u32[]{:S(2)}, u32[]{:S(2)}) collective-permute-start(s16[16,1664]{1,0:T(8,128)(2,1)S(1)} %get-tuple-element.44), channel_id=1, source_target_pairs={{0,6},{2,4},{4,2},{6,0},{1,7},{3,5},{5,3},{7,1},{8,14},{10,12},{12... | collective-permute-start | bytes 159752 | tf_op jit(solution)/shard_map/ppermute | solution.py:23

commit v2 on v1

v2 whole, which is shorter than its diff:
```python
import functools
import math

import jax
import jax.numpy as jnp
from jax import lax
from jax.experimental import pallas as pl
from jax.experimental.pallas import tpu as pltpu
from jax.sharding import PartitionSpec as P

LANES = 128
TOP = 32700.0
KEPT = 5
DEPENDS = 1
CUT = 5
STEPS = 4.0 / math.log(2.0)
VMEM = pl.BlockSpec(memory_space=pltpu.VMEM)
ANY = pl.BlockSpec(memory_space=pl.ANY)
HBM = pl.BlockSpec(memory_space=pltpu.HBM)


def peer(i, k, n):
    return i ^ k if n & (n - 1) == 0 else (i + k) % n


def send(array, axis, k, n):
    return lax.ppermute(array, axis, [(i, peer(i, k, n)) for i in range(n)])


def fetch(array, axis, k, n):
    return lax.ppermute(array, axis, [(peer(i, k, n), i) for i in range(n)])


def level(high):
    return jnp.ceil(jnp.log(jnp.maximum(high, 1e-30)) * STEPS)


def codes_of(x):
    steps = level(jnp.max(jnp.abs(x), axis=1, keepdims=True))
    y = x * (TOP * TOP * jnp.exp(steps * (-1.0 / STEPS)))
    return jnp.round(y * lax.rsqrt(jnp.abs(y) + 1e-20)), steps


def short(x):
    return x.astype(jnp.int32).astype(jnp.int16)


def wide(x):
    return x.astype(jnp.int32).astype(jnp.float32)


def values_of(code, steps):
    return code * jnp.abs(code) * (jnp.exp(steps * (1.0 / STEPS)) * (1.0 / (TOP * TOP)))


def encode(x, out_ref):
    rows, width = x.shape
    code, steps = codes_of(x)
    out_ref[:, :width] = short(code)
    out_ref[:, width:] = short(jnp.broadcast_to(steps, (rows, LANES)))


def decode(ref):
    width = ref.shape[1] - LANES
    return values_of(wide(ref[:, :width]), wide(ref[:, width:])[:, :1])


def folded(rows, width):
    if rows == 12 and width % (4 * LANES) == 0:
        return 16, width * 3 // 4 + LANES
    return -(-rows // 16) * 16, width + LANES


def fold(x, out_ref, work):
    rows, width = x.shape
    tall, main = out_ref.shape[0], out_ref.shape[1] - LANES
    code, steps = codes_of(x)
    work[:rows, :main] = code[:, :main]
    if tall > rows and main < width:
        part = width - main
        for i in range(rows):
            below, at = rows + i // 3, i % 3 * part
            work[below : below + 1, at : at + part] = code[i : i + 1, main:]
    elif tall > rows:
        work[rows:tall, :main] = jnp.zeros((tall - rows, main), jnp.float32)
    out_ref[:, :main] = short(work[:tall, :main])
    work[:rows, :LANES] = jnp.broadcast_to(steps, (rows, LANES))
    out_ref[:, main:] = short(work[:tall, :LANES])


def unfold(ref, rows, width, work):
    tall, main = ref.shape[0], ref.shape[1] - LANES
    code = wide(ref[:, :main])
    work[:rows, :main] = code[:rows]
    if main < width:
        part = width - main
        for i in range(rows):
            below, at = rows + i // 3, i % 3 * part
            work[i : i + 1, main:width] = code[below : below + 1, at : at + part]
    return values_of(work[:rows, :width], wide(ref[:, main:])[:rows, :1])


def ahead_kernel(plan, tn, w_ref, *refs):
    small_refs, fac_ref, kept_refs, rest = refs[:5], refs[5], refs[6 : 6 + len(plan)], refs[6 + len(plan) :]
    gap_rows, sem, small_sem, smalls = rest[0], rest[1], rest[2], rest[3:]
    gaps, omegas, weights, slots, blocks = smalls
    members, rows = fac_ref.shape[:2]
    small_copies = [pltpu.make_async_copy(a, b, small_sem.at[i]) for i, (a, b) in enumerate(zip(small_refs, smalls))]
    for c in small_copies:
        c.start()
    copies = []
    for (start, count), kept in zip(plan, kept_refs, strict=True):
        for i in range(count):
            column = start + i // members * tn
            source = w_ref.at[i % members, :, pl.ds(column, tn)]
            copies.append(pltpu.make_async_copy(source, kept.at[i], sem.at[len(copies)]))
            copies[-1].start()
    for c in small_copies:
        c.wait()
    me, groups = lax.axis_index("freq"), lax.axis_size("freq")
    blocks_all = blocks.shape[0]
    per, each = blocks_all // groups, rows // blocks_all
    for k in range(groups):
        place = peer(me, k, groups) * per

        def fill(q, carry):
            first = blocks[place + q] * each
            for i in range(each):
                row = (k * per + q) * each + i
                gap_rows[pl.ds(row, 1), :] = jnp.full((1, LANES), gaps[first + i], jnp.float32)
            return carry

        lax.fori_loop(0, per, fill, 0)
    gap = gap_rows[...]
    for m in range(members):
        slot = slots[me * members + m]
        omega = jnp.full((1, LANES), omegas[slot], jnp.float32)
        weight = jnp.full((1, LANES), weights[slot], jnp.float32)
        fac_ref[m] = weight * 2.0 * gap / (gap * gap + omega * omega)
    for c in copies:
        c.wait()


def ahead(screened, smalls, rows, plan, tn):
    members, depth, _ = screened.shape
    total = sum(count for _, count in plan)
    outs = [jax.ShapeDtypeStruct((members, rows, LANES), jnp.float32)]
    outs += [pltpu.VMEM((count, depth, tn), screened.dtype) for _, count in plan]
    return pl.pallas_call(
        functools.partial(ahead_kernel, plan, tn),
        in_specs=[HBM] * (1 + len(smalls)),
        out_specs=[VMEM] + [ANY] * len(plan),
        out_shape=outs,
        scratch_shapes=[
            pltpu.VMEM((rows, LANES), jnp.float32),
            pltpu.SemaphoreType.DMA((total,)),
            pltpu.SemaphoreType.DMA((len(smalls),)),
        ]
        + [pltpu.SMEM(a.shape, a.dtype) for a in smalls],
        compiler_params=pltpu.CompilerParams(vmem_limit_bytes=2 << 20),
        cost_estimate=pl.CostEstimate(flops=0, bytes_accessed=2 * total * depth * tn, transcendentals=0),
        name="pieces_ahead",
    )(screened, *(pltpu.with_memory_space_constraint(a, pltpu.HBM) for a in smalls))


def chunk_kernel(groups, start, tn, ring, after, *refs):
    b_refs, (fac_ref, kept_ref, w_ref), rest = refs[:groups], refs[groups : groups + 3], refs[groups + 3 + after :]
    own_ref, msg_refs, (all_rows, acc, buf, sem) = rest[0], rest[1:groups], rest[groups:]
    members = w_ref.shape[0]
    rows, width = own_ref.shape
    kept = kept_ref.shape[0]
    pieces = members * (width // tn)
    ring = min(ring, pieces - kept)

    def copy(i, slot):
        column = pl.multiple_of(start + lax.div(i, members) * tn, tn)
        return pltpu.make_async_copy(
            w_ref.at[lax.rem(i, members), :, pl.ds(column, tn)], buf.at[slot], sem.at[slot]
        )

    def add(i, matrix):
        member = lax.rem(i, members)
        product = jnp.dot(all_rows[...], matrix, preferred_element_type=jnp.float32)
        scaled = product * jnp.tile(fac_ref[member], (1, tn // LANES))
        columns = pl.ds(pl.multiple_of(lax.div(i, members) * tn, tn), tn)

        @pl.when(member == 0)
        def _():
            acc[:, columns] = scaled

        @pl.when(member > 0)
        def _():
            acc[:, columns] += scaled

    for i in range(ring):
        copy(kept + i, i).start()
    for k in range(groups):
        all_rows[k * rows : (k + 1) * rows, :] = b_refs[k][...]

    def early(i, carry):
        add(i, kept_ref[i])
        return carry

    def piece(i, carry):
        slot = lax.rem(i - kept, ring)
        copy(i, slot).wait()
        add(i, buf[slot])

        @pl.when(i + ring < pieces)
        def _():
            copy(i + ring, slot).start()

        return carry

    lax.fori_loop(0, kept, early, 0)
    if pieces > kept:
        lax.fori_loop(kept, pieces, piece, 0)
    own_ref[...] = acc[:rows, :]
    for k in range(1, groups):
        encode(acc[k * rows : (k + 1) * rows, :], msg_refs[k - 1])


def chunk(blocks, factor, kept, screened, start, width, tn, after):
    groups, (rows, depth) = len(blocks), blocks[0].shape
    members = screened.shape[0]
    ring = 4
    outs = [jax.ShapeDtypeStruct((rows, width), jnp.float32)]
    outs += [jax.ShapeDtypeStruct((rows, width + LANES), jnp.int16)] * (groups - 1)
    return pl.pallas_call(
        functools.partial(chunk_kernel, groups, start, tn, ring, len(after)),
        in_specs=[VMEM] * (groups + 2) + [ANY] * (1 + len(after)),
        out_specs=[VMEM] * groups,
        out_shape=outs,
        scratch_shapes=[
            pltpu.VMEM((groups * rows, depth), jnp.bfloat16),
            pltpu.VMEM((groups * rows, width), jnp.float32),
            pltpu.VMEM((ring, depth, tn), jnp.bfloat16),
            pltpu.SemaphoreType.DMA((ring,)),
        ],
        compiler_params=pltpu.CompilerParams(vmem_limit_bytes=20 << 20),
        cost_estimate=pl.CostEstimate(
            flops=2 * groups * rows * depth * width * members,
            bytes_accessed=2 * members * depth * width,
            transcendentals=0,
        ),
        name="weighted_products",
    )(*blocks, factor, kept, screened, *after)


def middle_kernel(groups, members, widths, after, *refs):
    chunks = len(widths)
    in_refs, (mine_ref, *out_refs) = refs[: chunks * groups], refs[chunks * groups + after : -3]
    total, picked, work = refs[-3:]
    rows, start = total.shape[0], 0
    each = rows // members
    for c, width in enumerate(widths):
        own_ref, *got_refs = in_refs[c * groups : (c + 1) * groups]
        x = own_ref[...]
        for ref in got_refs:
            x = x + decode(ref)
        total[:, start : start + width] = x
        start += width
    me = lax.axis_index("row")
    for target in range(members):
        for k in range(members):

            @pl.when(peer(me, k, members) == target)
            def _():
                picked[k] = total[target * each : (target + 1) * each, :]

    mine_ref[...] = picked[0]
    for k in range(1, members):
        fold(picked[k], out_refs[k - 1], work)


def middle(chunks, members, after):
    widths = [c[0].shape[1] for c in chunks]
    rows, width = chunks[0][0].shape[0], sum(widths)
    each = rows // members
    shape = folded(each, width)
    outs = [jax.ShapeDtypeStruct((each, width), jnp.float32)]
    outs += [jax.ShapeDtypeStruct(shape, jnp.int16)] * (members - 1)
    flat = [a for c in chunks for a in c]
    return pl.pallas_call(
        functools.partial(middle_kernel, len(chunks[0]), members, widths, len(after)),
        in_specs=[VMEM] * len(flat) + [ANY] * len(after),
        out_specs=[VMEM] * members,
        out_shape=outs,
        scratch_shapes=[
            pltpu.VMEM((rows, width), jnp.float32),
            pltpu.VMEM((members, each, width), jnp.float32),
            pltpu.VMEM(shape, jnp.float32),
        ],
        compiler_params=pltpu.CompilerParams(vmem_limit_bytes=24 << 20),
        name="frequency_sums",
    )(*flat, *after)


def last_kernel(widths, members, *refs):
    out_ref, work = refs[-2:]
    rows, start = out_ref.shape[0], 0
    for c, width in enumerate(widths):
        mine_ref, *got_refs = refs[c * members : (c + 1) * members]
        x = mine_ref[...]
        for ref in got_refs:
            x = x + unfold(ref, rows, width, work)
        out_ref[:, start : start + width] = x
        start += width


def last(parts, widths, members):
    rows = parts[0].shape[0]
    return pl.pallas_call(
        functools.partial(last_kernel, widths, members),
        in_specs=[VMEM] * len(parts),
        out_specs=VMEM,
        out_shape=jax.ShapeDtypeStruct((rows, sum(widths)), jnp.float32),
        scratch_shapes=[pltpu.VMEM((rows, max(widths)), jnp.float32)],
        compiler_params=pltpu.CompilerParams(vmem_limit_bytes=24 << 20),
        name="row_sums",
    )(*parts)


def split(columns, tn):
    units = columns // tn
    cuts = sorted({0, units * CUT // 8, units})
    return [(b - a) * tn for a, b in zip(cuts, cuts[1:])]


def local(pair_block, screened, pair_gaps, omega_values, quad_weight, freq_slot, block_list):
    groups, members = lax.axis_size("freq"), lax.axis_size("row")
    slots, _, columns = screened.shape
    tn = math.gcd(columns, 512)
    blocks = [pair_block] + [fetch(pair_block, "freq", k, groups) for k in range(1, groups)]
    widths = split(columns, tn)
    starts = [sum(widths[:c]) for c in range(len(widths))]
    plan = [(start, min(KEPT, width // tn * slots)) for start, width in zip(starts, widths)]
    smalls = (pair_gaps, omega_values, quad_weight, freq_slot, block_list)
    factor, *kept = ahead(screened, smalls, groups * pair_block.shape[0], plan, tn)
    made, after = [], []
    for c, width in enumerate(widths):
        made.append(chunk(blocks, factor, kept[c], screened, starts[c], width, tn, after))
        after = [made[-1][0]]
    sums = [[own] + [send(m, "freq", k + 1, groups) for k, m in enumerate(out)] for own, *out in made]
    parts, lasts = [], []
    for some in (sums[:-1], sums[-1:]):
        if some:
            mine, *out = middle(some, members, after)
            parts += [mine] + [send(m, "row", k + 1, members) for k, m in enumerate(out)]
            lasts.append(mine.shape[1])
            after = parts[-members + 1 :][:DEPENDS]
    return last(parts, lasts, members)


def solution(mesh):
    placed = (P("freq", "row"), P("freq", "row", "col"), P(), P(), P(), P(), P())
    return jax.shard_map(
        local, mesh=mesh, in_specs=placed, out_specs=P(("freq", "row"), "col"), check_vma=False
    )
```

time: 78.2 us -> 59.9 us (0.77)
  waiting for transfers between devices: 15.7 us -> 6.94 us
  starting transfers between devices: 28.1 us -> 22.2 us
  local copies, waits for them, and re-layouts: 2.83 us -> 0.01 us
  other arithmetic: 2.07 us -> 0 us
  Pallas kernels: 29.1 us -> 30.6 us
    ppermute x18 -> x12, starting transfers between devices: 23.7 us -> 17.7 us  [send(): return lax.ppermute(array, axis, [(i, peer(i, k, n)) for i in range(n)])]
    ppermute x18 -> x12, waiting for transfers between devices: 10.3 us -> 5.29 us  [send(): return lax.ppermute(array, axis, [(i, peer(i, k, n)) for i in range(n)])]
    ppermute x3, waiting for transfers between devices: 5.39 us -> 1.65 us  [fetch(): return lax.ppermute(array, axis, [(peer(i, k, n), i) for i in range(n)])]
    reduce_sum x3 -> x0, other arithmetic: 1.82 us -> none  [the longest x1 0.88 us: factors(): jnp.sum(jnp.where(match, quad_weight[None, :], 0.0), axis=1)[:, None]]
    pallas_call x6 -> x5, Pallas kernels: 28.3 us -> 29.7 us  [the longest x2 21 us: chunk(): pl.pallas_call(functools.partial(chunk_kernel, groups, start, tn, ring, l...]
    broadcast_in_dim x3 -> x0, local copies, waits for them, and re-layouts: 1 us -> none  [the longest x2 0.84 us: factors(): jnp.where((blocks[:, None] == every[None, :])[:, :, None], gap_table[None...]
    unnamed x2, local copies, waits for them, and re-layouts: 0.93 us -> 0.01 us
  transfers between devices with their start and end apart: 21 -> 15, of which waited for: 5 -> 6; matrix products, arithmetic and copies ran while one was open for 5% -> 0% of each run, Pallas kernels for 31% -> 28%
where the time goes in v2:
time: 59.9 us; the launch traced here: 59.8 us
  Pallas kernels  30.6 us (51%)
  starting transfers between devices  22.2 us (37%)
  waiting for transfers between devices  6.94 us (12%)
    pallas_call x2, Pallas kernels, chunk(): pl.pallas_call(functools.partial(chunk_kernel, groups, start, tn, ring, l...  21 us
    ppermute x12, starting transfers between devices, send(): return lax.ppermute(array, axis, [(i, peer(i, k, n)) for i in range(n)])  17.7 us
    pallas_call x1, Pallas kernels, ahead(): pl.pallas_call(functools.partial(ahead_kernel, plan, tn), in_specs=[HBM]...  7.32 us
    ppermute x12, waiting for transfers between devices, send(): return lax.ppermute(array, axis, [(i, peer(i, k, n)) for i in range(n)])  5.29 us
    ppermute x3, starting transfers between devices, fetch(): return lax.ppermute(array, axis, [(peer(i, k, n), i) for i in range(n)])  4.52 us
    ppermute x3, waiting for transfers between devices, fetch(): return lax.ppermute(array, axis, [(peer(i, k, n), i) for i in range(n)])  1.65 us
    pallas_call x2, Pallas kernels, middle(): pl.pallas_call(functools.partial(middle_kernel, len(chunks[0]), members,...  1.4 us
  transfers between devices with their start and end apart: 15, of which 6 were waited for; matrix products, arithmetic and copies ran while one was open for 0% of the time, Pallas kernels for 28%

profile of v2, /device:TPU:0, one launch (start us, length us, event | category | flops | bytes accessed | tf_op | source)
XLA Modules:
  0.0 59.8 jit_solution(6077016965461271766)
XLA Ops:
  0.0 0.0 copy-start
  0.0 3.9 %collective-permute-start.2 = (bf16[48,2048]{1,0:T(8,128)(2,1)}, bf16[48,2048]{1,0:T(8,128)(2,1)S(1)}, u32[]{:S(2)}, u32[]{:S(2)}) collective-permute-start(bf16[48,2048]{1,0:T(8,128)(2,1)} %refs_0_.5), channel_id=1, source_target_pairs={{24,0},{16,8},{8,16},{0,24},{25,1},{17,9},{9,17},{1,25},{26,2},{18... | collective-permute-start | bytes 589832 | tf_op jit(solution)/shard_map/ppermute | solution.py:31
  3.9 0.5 collective-permute-start.1
  4.4 0.1 collective-permute-start
  4.5 7.3 %pieces_ahead.1 = (f32[4,192,128]{2,1,0:T(8,128)S(1)}, bf16[5,2048,512]{2,1,0:T(8,128)(2,1)S(1)}, bf16[5,2048,512]{2,1,0:T(8,128)(2,1)S(1)}) custom-call(bf16[4,2048,4096]{2,1,0:T(8,128)(2,1)} %refs_6_.3, f32[192]{0:T(256)} %refs_0_.3, f32[16]{0:T(128)} %refs_1_.1, f32[16]{0:T(128)} %refs_2_.1, s32[16]{0:T(128)} %refs_3_.1, s32[16]{0:T(128)} %refs_4_.1), custom_call_target="tpu_custom_call" | custom-call | bytes 20971520 | tf_op jit(solution)/shard_map/pieces_ahead/pallas_call | solution.py:149
  11.9 0.0 collective-permute-done.2.refs_3_
  11.9 1.4 %collective-permute-done.1.refs_2_ = bf16[48,2048]{1,0:T(8,128)(2,1)S(1)} collective-permute-done((bf16[48,2048]{1,0:T(8,128)(2,1)}, bf16[48,2048]{1,0:T(8,128)(2,1)S(1)}, u32[]{:S(2)}, u32[]{:S(2)}) %collective-permute-start.1) | collective-permute-done | bytes 196640 | tf_op jit(solution)/shard_map/ppermute | solution.py:31
  13.3 0.2 collective-permute-done.refs_1_
  13.5 0.0 copy-done
  13.5 13.1 %weighted_products.2 = (f32[48,2560]{1,0:T(8,128)S(1)}, s16[48,2688]{1,0:T(8,128)(2,1)S(1)}, s16[48,2688]{1,0:T(8,128)(2,1)S(1)}, s16[48,2688]{1,0:T(8,128)(2,1)S(1)}) custom-call(bf16[48,2048]{1,0:T(8,128)(2,1)S(1)} %copy-done, bf16[48,2048]{1,0:T(8,128)(2,1)S(1)} %collective-permute-done.refs_1_, bf16[48,2048]{1,0:T(8,128)(2,1)S(1)} %collective-permute-done.1.refs_2_, ...), custom_call_target="tpu_custom_call" | custom-call | flops 8053063680 | bytes 41943040 | tf_op jit(solution)/shard_map/weighted_products/pallas_call | solution.py:229
  26.6 1.5 %collective-permute-start.3 = (s16[48,2688]{1,0:T(8,128)(2,1)S(1)}, s16[48,2688]{1,0:T(8,128)(2,1)S(1)}, u32[]{:S(2)}, u32[]{:S(2)}) collective-permute-start(s16[48,2688]{1,0:T(8,128)(2,1)S(1)} %get-tuple-element.27), channel_id=1, source_target_pairs={{0,8},{8,0},{16,24},{24,16},{1,9},{9,1},{17,25},{25,17},{2,10},{10... | collective-permute-start | bytes 774152 | tf_op jit(solution)/shard_map/ppermute | solution.py:27
  28.1 0.6 collective-permute-start.4
  28.7 1.5 %collective-permute-start.5 = (s16[48,2688]{1,0:T(8,128)(2,1)S(1)}, s16[48,2688]{1,0:T(8,128)(2,1)S(1)}, u32[]{:S(2)}, u32[]{:S(2)}) collective-permute-start(s16[48,2688]{1,0:T(8,128)(2,1)S(1)} %get-tuple-element.29), channel_id=1, source_target_pairs={{0,24},{8,16},{16,8},{24,0},{1,25},{9,17},{17,9},{25,1},{2,26},{10... | collective-permute-start | bytes 774152 | tf_op jit(solution)/shard_map/ppermute | solution.py:27
  30.2 7.9 %weighted_products.3 = (f32[48,1536]{1,0:T(8,128)S(1)}, s16[48,1664]{1,0:T(8,128)(2,1)S(1)}, s16[48,1664]{1,0:T(8,128)(2,1)S(1)}, s16[48,1664]{1,0:T(8,128)(2,1)S(1)}) custom-call(bf16[48,2048]{1,0:T(8,128)(2,1)S(1)} %copy-done, bf16[48,2048]{1,0:T(8,128)(2,1)S(1)} %collective-permute-done.refs_1_, bf16[48,2048]{1,0:T(8,128)(2,1)S(1)} %collective-permute-done.1.refs_2_, ...), custom_call_target="tpu_custom_call" | custom-call | flops 4831838208 | bytes 25165824 | tf_op jit(solution)/shard_map/weighted_products/pallas_call | solution.py:229
  38.0 1.5 %collective-permute-start.9 = (s16[48,1664]{1,0:T(8,128)(2,1)S(1)}, s16[48,1664]{1,0:T(8,128)(2,1)S(1)}, u32[]{:S(2)}, u32[]{:S(2)}) collective-permute-start(s16[48,1664]{1,0:T(8,128)(2,1)S(1)} %get-tuple-element.36), channel_id=1, source_target_pairs={{0,8},{8,0},{16,24},{24,16},{1,9},{9,1},{17,25},{25,17},{2,10},{10... | collective-permute-start | bytes 479240 | tf_op jit(solution)/shard_map/ppermute | solution.py:27
  39.5 0.6 collective-permute-start.10
  40.1 0.0 collective-permute-done.3.refs_1_
  40.1 1.5 %collective-permute-start.11 = (s16[48,1664]{1,0:T(8,128)(2,1)S(1)}, s16[48,1664]{1,0:T(8,128)(2,1)S(1)}, u32[]{:S(2)}, u32[]{:S(2)}) collective-permute-start(s16[48,1664]{1,0:T(8,128)(2,1)S(1)} %get-tuple-element.38), channel_id=1, source_target_pairs={{0,24},{8,16},{16,8},{24,0},{1,25},{9,17},{17,9},{25,1},{2,26},{10... | collective-permute-start | bytes 479240 | tf_op jit(solution)/shard_map/ppermute | solution.py:27
  41.6 0.0 collective-permute-done.4.refs_2_
  41.6 0.1 collective-permute-done.5.refs_3_
  41.7 0.9 %frequency_sums.2 = (f32[12,2560]{1,0:T(8,128)S(1)}, s16[16,2048]{1,0:T(8,128)(2,1)S(1)}, s16[16,2048]{1,0:T(8,128)(2,1)S(1)}, s16[16,2048]{1,0:T(8,128)(2,1)S(1)}) custom-call(f32[48,2560]{1,0:T(8,128)S(1)} %get-tuple-element.26.refs_7_.refs_0_, s16[48,2688]{1,0:T(8,128)(2,1)S(1)} %collective-permute-done.3.refs_1_, ...), custom_call_target="tpu_custom_call" | custom-call | tf_op jit(solution)/shard_map/frequency_sums/pallas_call | solution.py:284
  42.6 1.6 %collective-permute-start.6 = (s16[16,2048]{1,0:T(8,128)(2,1)S(1)}, s16[16,2048]{1,0:T(8,128)(2,1)S(1)}, u32[]{:S(2)}, u32[]{:S(2)}) collective-permute-start(s16[16,2048]{1,0:T(8,128)(2,1)S(1)} %get-tuple-element.33), channel_id=1, source_target_pairs={{0,2},{2,0},{4,6},{6,4},{1,3},{3,1},{5,7},{7,5},{8,10},{10,8},{12,... | collective-permute-start | bytes 196616 | tf_op jit(solution)/shard_map/ppermute | solution.py:27
  44.2 2.5 %collective-permute-start.7 = (s16[16,2048]{1,0:T(8,128)(2,1)S(1)}, s16[16,2048]{1,0:T(8,128)(2,1)S(1)}, u32[]{:S(2)}, u32[]{:S(2)}) collective-permute-start(s16[16,2048]{1,0:T(8,128)(2,1)S(1)} %get-tuple-element.34), channel_id=1, source_target_pairs={{0,4},{2,6},{4,0},{6,2},{1,5},{3,7},{5,1},{7,3},{8,12},{10,14},{12... | collective-permute-start | bytes 196616 | tf_op jit(solution)/shard_map/ppermute | solution.py:27
  46.8 0.0 collective-permute-done.9.refs_1_
  46.8 1.9 %collective-permute-start.8 = (s16[16,2048]{1,0:T(8,128)(2,1)S(1)}, s16[16,2048]{1,0:T(8,128)(2,1)S(1)}, u32[]{:S(2)}, u32[]{:S(2)}) collective-permute-start(s16[16,2048]{1,0:T(8,128)(2,1)S(1)} %get-tuple-element.35), channel_id=1, source_target_pairs={{0,6},{2,4},{4,2},{6,0},{1,7},{3,5},{5,3},{7,1},{8,14},{10,12},{12... | collective-permute-start | bytes 196616 | tf_op jit(solution)/shard_map/ppermute | solution.py:27
  48.7 0.0 collective-permute-done.10.refs_2_
  48.7 0.0 collective-permute-done.11.refs_3_
  48.7 0.0 collective-permute-done.6.refs_4_.refs_1_
  48.7 0.5 frequency_sums.3
  49.2 1.2 %collective-permute-start.12 = (s16[16,1280]{1,0:T(8,128)(2,1)S(1)}, s16[16,1280]{1,0:T(8,128)(2,1)S(1)}, u32[]{:S(2)}, u32[]{:S(2)}) collective-permute-start(s16[16,1280]{1,0:T(8,128)(2,1)S(1)} %get-tuple-element.40), channel_id=1, source_target_pairs={{0,2},{2,0},{4,6},{6,4},{1,3},{3,1},{5,7},{7,5},{8,10},{10,8},{12,... | collective-permute-start | bytes 122888 | tf_op jit(solution)/shard_map/ppermute | solution.py:27
  50.5 2.6 %collective-permute-start.13 = (s16[16,1280]{1,0:T(8,128)(2,1)S(1)}, s16[16,1280]{1,0:T(8,128)(2,1)S(1)}, u32[]{:S(2)}, u32[]{:S(2)}) collective-permute-start(s16[16,1280]{1,0:T(8,128)(2,1)S(1)} %get-tuple-element.41), channel_id=1, source_target_pairs={{0,4},{2,6},{4,0},{6,2},{1,5},{3,7},{5,1},{7,3},{8,12},{10,14},{12... | collective-permute-start | bytes 122888 | tf_op jit(solution)/shard_map/ppermute | solution.py:27
  53.0 0.6 %collective-permute-start.14 = (s16[16,1280]{1,0:T(8,128)(2,1)S(1)}, s16[16,1280]{1,0:T(8,128)(2,1)S(1)}, u32[]{:S(2)}, u32[]{:S(2)}) collective-permute-start(s16[16,1280]{1,0:T(8,128)(2,1)S(1)} %get-tuple-element.42), channel_id=1, source_target_pairs={{0,6},{2,4},{4,2},{6,0},{1,7},{3,5},{5,3},{7,1},{8,14},{10,12},{12... | collective-permute-start | bytes 122888 | tf_op jit(solution)/shard_map/ppermute | solution.py:27
  53.7 0.0 collective-permute-done.7.refs_2_
  53.7 0.0 collective-permute-done.8.refs_3_
  53.7 0.1 collective-permute-done.12.refs_5_
  53.8 2.5 %collective-permute-done.13.refs_6_ = s16[16,1280]{1,0:T(8,128)(2,1)S(1)} collective-permute-done((s16[16,1280]{1,0:T(8,128)(2,1)S(1)}, s16[16,1280]{1,0:T(8,128)(2,1)S(1)}, u32[]{:S(2)}, u32[]{:S(2)}) %collective-permute-start.13) | collective-permute-done | bytes 40992 | tf_op jit(solution)/shard_map/ppermute | solution.py:27
  56.3 2.6 %collective-permute-done.14.refs_7_ = s16[16,1280]{1,0:T(8,128)(2,1)S(1)} collective-permute-done((s16[16,1280]{1,0:T(8,128)(2,1)S(1)}, s16[16,1280]{1,0:T(8,128)(2,1)S(1)}, u32[]{:S(2)}, u32[]{:S(2)}) %collective-permute-start.14) | collective-permute-done | bytes 40992 | tf_op jit(solution)/shard_map/ppermute | solution.py:27
  58.8 1.0 %row_sums.1 = f32[12,4096]{1,0:T(8,128)} custom-call(f32[12,2560]{1,0:T(8,128)S(1)} %get-tuple-element.32.refs_0_, s16[16,2048]{1,0:T(8,128)(2,1)S(1)} %collective-permute-done.6.refs_4_.refs_1_, s16[16,2048]{1,0:T(8,128)(2,1)S(1)} %collective-permute-done.7.refs_2_, s16[16,2048]{1,0:T(8,128)(2,1)S(1)} %collective-permute-done.8.refs_3_, ...), custom_call_target="tpu_custom_call" | custom-call | tf_op jit(solution)/shard_map/row_sums/pallas_call | solution.py:313
Async XLA Ops:
  0.0 13.5 %copy-start = (bf16[48,2048]{1,0:T(8,128)(2,1)S(1)}, bf16[48,2048]{1,0:T(8,128)(2,1)}, u32[]{:S(2)}) copy-start(bf16[48,2048]{1,0:T(8,128)(2,1)} %refs_0_.5) | copy-start | bytes 589828
  0.0 11.9 %collective-permute-start.2 = (bf16[48,2048]{1,0:T(8,128)(2,1)}, bf16[48,2048]{1,0:T(8,128)(2,1)S(1)}, u32[]{:S(2)}, u32[]{:S(2)}) collective-permute-start(bf16[48,2048]{1,0:T(8,128)(2,1)} %refs_0_.5), channel_id=1, source_target_pairs={{24,0},{16,8},{8,16},{0,24},{25,1},{17,9},{9,17},{1,25},{26,2},{18... | collective-permute-start | bytes 589832 | tf_op jit(solution)/shard_map/ppermute | solution.py:31
  3.9 9.4 %collective-permute-start.1 = (bf16[48,2048]{1,0:T(8,128)(2,1)}, bf16[48,2048]{1,0:T(8,128)(2,1)S(1)}, u32[]{:S(2)}, u32[]{:S(2)}) collective-permute-start(bf16[48,2048]{1,0:T(8,128)(2,1)} %refs_0_.5), channel_id=1, source_target_pairs={{16,0},{24,8},{0,16},{8,24},{17,1},{25,9},{1,17},{9,25},{18,2},{26... | collective-permute-start | bytes 589832 | tf_op jit(solution)/shard_map/ppermute | solution.py:31
  4.4 9.1 %collective-permute-start = (bf16[48,2048]{1,0:T(8,128)(2,1)}, bf16[48,2048]{1,0:T(8,128)(2,1)S(1)}, u32[]{:S(2)}, u32[]{:S(2)}) collective-permute-start(bf16[48,2048]{1,0:T(8,128)(2,1)} %refs_0_.5), channel_id=1, source_target_pairs={{8,0},{0,8},{24,16},{16,24},{9,1},{1,9},{25,17},{17,25},{10,2},{2,... | collective-permute-start | bytes 589832 | tf_op jit(solution)/shard_map/ppermute | solution.py:31
  26.6 13.5 %collective-permute-start.3 = (s16[48,2688]{1,0:T(8,128)(2,1)S(1)}, s16[48,2688]{1,0:T(8,128)(2,1)S(1)}, u32[]{:S(2)}, u32[]{:S(2)}) collective-permute-start(s16[48,2688]{1,0:T(8,128)(2,1)S(1)} %get-tuple-element.27), channel_id=1, source_target_pairs={{0,8},{8,0},{16,24},{24,16},{1,9},{9,1},{17,25},{25,17},{2,10},{10... | collective-permute-start | bytes 774152 | tf_op jit(solution)/shard_map/ppermute | solution.py:27
  28.1 13.5 %collective-permute-start.4 = (s16[48,2688]{1,0:T(8,128)(2,1)S(1)}, s16[48,2688]{1,0:T(8,128)(2,1)S(1)}, u32[]{:S(2)}, u32[]{:S(2)}) collective-permute-start(s16[48,2688]{1,0:T(8,128)(2,1)S(1)} %get-tuple-element.28), channel_id=1, source_target_pairs={{0,16},{8,24},{16,0},{24,8},{1,17},{9,25},{17,1},{25,9},{2,18},{10... | collective-permute-start | bytes 774152 | tf_op jit(solution)/shard_map/ppermute | solution.py:27
  28.7 13.0 %collective-permute-start.5 = (s16[48,2688]{1,0:T(8,128)(2,1)S(1)}, s16[48,2688]{1,0:T(8,128)(2,1)S(1)}, u32[]{:S(2)}, u32[]{:S(2)}) collective-permute-start(s16[48,2688]{1,0:T(8,128)(2,1)S(1)} %get-tuple-element.29), channel_id=1, source_target_pairs={{0,24},{8,16},{16,8},{24,0},{1,25},{9,17},{17,9},{25,1},{2,26},{10... | collective-permute-start | bytes 774152 | tf_op jit(solution)/shard_map/ppermute | solution.py:27
  38.0 8.7 %collective-permute-start.9 = (s16[48,1664]{1,0:T(8,128)(2,1)S(1)}, s16[48,1664]{1,0:T(8,128)(2,1)S(1)}, u32[]{:S(2)}, u32[]{:S(2)}) collective-permute-start(s16[48,1664]{1,0:T(8,128)(2,1)S(1)} %get-tuple-element.36), channel_id=1, source_target_pairs={{0,8},{8,0},{16,24},{24,16},{1,9},{9,1},{17,25},{25,17},{2,10},{10... | collective-permute-start | bytes 479240 | tf_op jit(solution)/shard_map/ppermute | solution.py:27
  39.5 9.2 %collective-permute-start.10 = (s16[48,1664]{1,0:T(8,128)(2,1)S(1)}, s16[48,1664]{1,0:T(8,128)(2,1)S(1)}, u32[]{:S(2)}, u32[]{:S(2)}) collective-permute-start(s16[48,1664]{1,0:T(8,128)(2,1)S(1)} %get-tuple-element.37), channel_id=1, source_target_pairs={{0,16},{8,24},{16,0},{24,8},{1,17},{9,25},{17,1},{25,9},{2,18},{10... | collective-permute-start | bytes 479240 | tf_op jit(solution)/shard_map/ppermute | solution.py:27
  40.1 8.6 %collective-permute-start.11 = (s16[48,1664]{1,0:T(8,128)(2,1)S(1)}, s16[48,1664]{1,0:T(8,128)(2,1)S(1)}, u32[]{:S(2)}, u32[]{:S(2)}) collective-permute-start(s16[48,1664]{1,0:T(8,128)(2,1)S(1)} %get-tuple-element.38), channel_id=1, source_target_pairs={{0,24},{8,16},{16,8},{24,0},{1,25},{9,17},{17,9},{25,1},{2,26},{10... | collective-permute-start | bytes 479240 | tf_op jit(solution)/shard_map/ppermute | solution.py:27
  42.6 6.1 %collective-permute-start.6 = (s16[16,2048]{1,0:T(8,128)(2,1)S(1)}, s16[16,2048]{1,0:T(8,128)(2,1)S(1)}, u32[]{:S(2)}, u32[]{:S(2)}) collective-permute-start(s16[16,2048]{1,0:T(8,128)(2,1)S(1)} %get-tuple-element.33), channel_id=1, source_target_pairs={{0,2},{2,0},{4,6},{6,4},{1,3},{3,1},{5,7},{7,5},{8,10},{10,8},{12,... | collective-permute-start | bytes 196616 | tf_op jit(solution)/shard_map/ppermute | solution.py:27
  44.2 9.4 %collective-permute-start.7 = (s16[16,2048]{1,0:T(8,128)(2,1)S(1)}, s16[16,2048]{1,0:T(8,128)(2,1)S(1)}, u32[]{:S(2)}, u32[]{:S(2)}) collective-permute-start(s16[16,2048]{1,0:T(8,128)(2,1)S(1)} %get-tuple-element.34), channel_id=1, source_target_pairs={{0,4},{2,6},{4,0},{6,2},{1,5},{3,7},{5,1},{7,3},{8,12},{10,14},{12... | collective-permute-start | bytes 196616 | tf_op jit(solution)/shard_map/ppermute | solution.py:27
  46.8 6.9 %collective-permute-start.8 = (s16[16,2048]{1,0:T(8,128)(2,1)S(1)}, s16[16,2048]{1,0:T(8,128)(2,1)S(1)}, u32[]{:S(2)}, u32[]{:S(2)}) collective-permute-start(s16[16,2048]{1,0:T(8,128)(2,1)S(1)} %get-tuple-element.35), channel_id=1, source_target_pairs={{0,6},{2,4},{4,2},{6,0},{1,7},{3,5},{5,3},{7,1},{8,14},{10,12},{12... | collective-permute-start | bytes 196616 | tf_op jit(solution)/shard_map/ppermute | solution.py:27
  49.2 4.5 %collective-permute-start.12 = (s16[16,1280]{1,0:T(8,128)(2,1)S(1)}, s16[16,1280]{1,0:T(8,128)(2,1)S(1)}, u32[]{:S(2)}, u32[]{:S(2)}) collective-permute-start(s16[16,1280]{1,0:T(8,128)(2,1)S(1)} %get-tuple-element.40), channel_id=1, source_target_pairs={{0,2},{2,0},{4,6},{6,4},{1,3},{3,1},{5,7},{7,5},{8,10},{10,8},{12,... | collective-permute-start | bytes 122888 | tf_op jit(solution)/shard_map/ppermute | solution.py:27
  50.5 5.8 %collective-permute-start.13 = (s16[16,1280]{1,0:T(8,128)(2,1)S(1)}, s16[16,1280]{1,0:T(8,128)(2,1)S(1)}, u32[]{:S(2)}, u32[]{:S(2)}) collective-permute-start(s16[16,1280]{1,0:T(8,128)(2,1)S(1)} %get-tuple-element.41), channel_id=1, source_target_pairs={{0,4},{2,6},{4,0},{6,2},{1,5},{3,7},{5,1},{7,3},{8,12},{10,14},{12... | collective-permute-start | bytes 122888 | tf_op jit(solution)/shard_map/ppermute | solution.py:27
  53.0 5.8 %collective-permute-start.14 = (s16[16,1280]{1,0:T(8,128)(2,1)S(1)}, s16[16,1280]{1,0:T(8,128)(2,1)S(1)}, u32[]{:S(2)}, u32[]{:S(2)}) collective-permute-start(s16[16,1280]{1,0:T(8,128)(2,1)S(1)} %get-tuple-element.42), channel_id=1, source_target_pairs={{0,6},{2,4},{4,2},{6,0},{1,7},{3,5},{5,3},{7,1},{8,14},{10,12},{12... | collective-permute-start | bytes 122888 | tf_op jit(solution)/shard_map/ppermute | solution.py:27

commit v3 on v2

--- a/solution.py
+++ b/solution.py
@@ -10,9 +10,11 @@
 
 LANES = 128
 TOP = 32700.0
-KEPT = 5
+EARLY, NEXT, SPACE = 3, 2, 5
+UNIT = 256
+SUM_ROWS = 1024
 DEPENDS = 1
-CUT = 5
+CUT = 4
 STEPS = 4.0 / math.log(2.0)
 VMEM = pl.BlockSpec(memory_space=pltpu.VMEM)
 ANY = pl.BlockSpec(memory_space=pl.ANY)
@@ -25,6 +27,14 @@
 
 def send(array, axis, k, n):
     return lax.ppermute(array, axis, [(i, peer(i, k, n)) for i in range(n)])
+
+
+def order(n):
+    return list(range(n - 1, 0, -1))
+
+
+def send_all(arrays, axis, n):
+    return [send(a, axis, k, n) for k, a in zip(order(n), arrays)]
 
 
 def fetch(array, axis, k, n):
@@ -100,21 +110,26 @@
     return values_of(work[:rows, :width], wide(ref[:, main:])[:rows, :1])
 
 
-def ahead_kernel(plan, tn, w_ref, *refs):
-    small_refs, fac_ref, kept_refs, rest = refs[:5], refs[5], refs[6 : 6 + len(plan)], refs[6 + len(plan) :]
+def fetch_piece(w_ref, ring_ref, sem, i, tn):
+    members, slots = w_ref.shape[0], ring_ref.shape[0]
+    if isinstance(i, int):
+        member, column, slot = i % members, i // members * tn, i % slots
+    else:
+        member, column, slot = lax.rem(i, members), pl.multiple_of(lax.div(i, members) * tn, tn), lax.rem(i, slots)
+    return pltpu.make_async_copy(w_ref.at[member, :, pl.ds(column, tn)], ring_ref.at[slot], sem.at[slot])
+
+
+def ahead_kernel(count, tn, w_ref, *refs):
+    small_refs, fac_ref, ring_ref, rest = refs[:5], refs[5], refs[6], refs[7:]
     gap_rows, sem, small_sem, smalls = rest[0], rest[1], rest[2], rest[3:]
     gaps, omegas, weights, slots, blocks = smalls
     members, rows = fac_ref.shape[:2]
     small_copies = [pltpu.make_async_copy(a, b, small_sem.at[i]) for i, (a, b) in enumerate(zip(small_refs, smalls))]
     for c in small_copies:
         c.start()
-    copies = []
-    for (start, count), kept in zip(plan, kept_refs, strict=True):
-        for i in range(count):
-            column = start + i // members * tn
-            source = w_ref.at[i % members, :, pl.ds(column, tn)]
-            copies.append(pltpu.make_async_copy(source, kept.at[i], sem.at[len(copies)]))
-            copies[-1].start()
+    copies = [fetch_piece(w_ref, ring_ref, sem, i, tn) for i in range(count)]
+    for c in copies:
+        c.start()
     for c in small_copies:
         c.wait()
     me, groups = lax.axis_index("freq"), lax.axis_size("freq")
@@ -141,110 +156,140 @@
         c.wait()
 
 
-def ahead(screened, smalls, rows, plan, tn):
+def ahead(screened, smalls, rows, count, slots, tn):
     members, depth, _ = screened.shape
-    total = sum(count for _, count in plan)
-    outs = [jax.ShapeDtypeStruct((members, rows, LANES), jnp.float32)]
-    outs += [pltpu.VMEM((count, depth, tn), screened.dtype) for _, count in plan]
     return pl.pallas_call(
-        functools.partial(ahead_kernel, plan, tn),
+        functools.partial(ahead_kernel, count, tn),
         in_specs=[HBM] * (1 + len(smalls)),
-        out_specs=[VMEM] + [ANY] * len(plan),
-        out_shape=outs,
+        out_specs=[VMEM, ANY],
+        out_shape=[
+            jax.ShapeDtypeStruct((members, rows, LANES), jnp.float32),
+            pltpu.VMEM((slots, depth, tn), screened.dtype),
+        ],
         scratch_shapes=[
             pltpu.VMEM((rows, LANES), jnp.float32),
-            pltpu.SemaphoreType.DMA((total,)),
+            pltpu.SemaphoreType.DMA((slots,)),
             pltpu.SemaphoreType.DMA((len(smalls),)),
         ]
         + [pltpu.SMEM(a.shape, a.dtype) for a in smalls],
         compiler_params=pltpu.CompilerParams(vmem_limit_bytes=2 << 20),
-        cost_estimate=pl.CostEstimate(flops=0, bytes_accessed=2 * total * depth * tn, transcendentals=0),
+        cost_estimate=pl.CostEstimate(flops=0, bytes_accessed=2 * count * depth * tn, transcendentals=0),
         name="pieces_ahead",
     )(screened, *(pltpu.with_memory_space_constraint(a, pltpu.HBM) for a in smalls))
 
 
-def chunk_kernel(groups, start, tn, ring, after, *refs):
-    b_refs, (fac_ref, kept_ref, w_ref), rest = refs[:groups], refs[groups : groups + 3], refs[groups + 3 + after :]
-    own_ref, msg_refs, (all_rows, acc, buf, sem) = rest[0], rest[1:groups], rest[groups:]
-    members = w_ref.shape[0]
+def chunk_kernel(groups, first_tile, have, want, tn, *refs):
+    b_refs, (fac_ref, w_ref, _), rest = refs[:groups], refs[groups : groups + 3], refs[groups + 3 :]
+    own_ref, msg_refs, (ring_ref, all_rows, acc, sem) = rest[0], rest[1:groups], rest[groups:]
+    (members, depth, _), slots = w_ref.shape, ring_ref.shape[0]
     rows, width = own_ref.shape
-    kept = kept_ref.shape[0]
-    pieces = members * (width // tn)
-    ring = min(ring, pieces - kept)
-
-    def copy(i, slot):
-        column = pl.multiple_of(start + lax.div(i, members) * tn, tn)
-        return pltpu.make_async_copy(
-            w_ref.at[lax.rem(i, members), :, pl.ds(column, tn)], buf.at[slot], sem.at[slot]
-        )
-
-    def add(i, matrix):
-        member = lax.rem(i, members)
-        product = jnp.dot(all_rows[...], matrix, preferred_element_type=jnp.float32)
-        scaled = product * jnp.tile(fac_ref[member], (1, tn // LANES))
-        columns = pl.ds(pl.multiple_of(lax.div(i, members) * tn, tn), tn)
-
-        @pl.when(member == 0)
-        def _():
-            acc[:, columns] = scaled
-
-        @pl.when(member > 0)
-        def _():
-            acc[:, columns] += scaled
-
-    for i in range(ring):
-        copy(kept + i, i).start()
+    tiles = width // tn
+    begin, end = first_tile * members, (first_tile + tiles) * members
+
+    def copy(i):
+        return fetch_piece(w_ref, ring_ref, sem, i, tn)
+
+    def add(tile, place, sums):
+        units, per = len(sums), tn // UNIT // len(sums)
+        order = [(m, c, k) for m in range(members) for c in range(per) for k in range(depth // UNIT)]
+
+        def push(step):
+            m, c, k = order[step]
+            for u in range(units):
+                columns = slice((c * units + u) * UNIT, (c * units + u + 1) * UNIT)
+                piece = ring_ref[place + m, k * UNIT : (k + 1) * UNIT, columns]
+                pltpu.matmul_push_rhs(piece, step % 2, u)
+
+        def close(m, c):
+            for u in range(units):
+                product = pltpu.matmul_pop(sums[u][(m * per + c) % len(sums[u])])
+                scaled = product * jnp.tile(fac_ref[m], (1, UNIT // LANES))
+                column = pl.multiple_of(tile * tn + (c * units + u) * UNIT, UNIT)
+                if m == 0:
+                    acc[:, pl.ds(column, UNIT)] = scaled
+                else:
+                    acc[:, pl.ds(column, UNIT)] += scaled
+
+        push(0)
+        late = []
+        for step, (m, c, k) in enumerate(order):
+            if step + 1 < len(order):
+                push(step + 1)
+            for u in range(units):
+                part = all_rows[:, k * UNIT : (k + 1) * UNIT]
+                pltpu.matmul_acc_lhs(sums[u][(m * per + c) % len(sums[u])], part, load_staged_rhs=step % 2)
+            if late and step >= late[0][0]:
+                close(*late.pop(0)[1:])
+            if k + 1 == depth // UNIT:
+                late.append((step + min(3, depth // UNIT - 1), m, c))
+                if len(sums[0]) == 1:
+                    close(*late.pop()[1:])
+        for _, m, c in late:
+            close(m, c)
+
+    for i in range(have, min(want, begin + slots)):
+        copy(i).start()
     for k in range(groups):
         all_rows[k * rows : (k + 1) * rows, :] = b_refs[k][...]
-
-    def early(i, carry):
-        add(i, kept_ref[i])
-        return carry
-
-    def piece(i, carry):
-        slot = lax.rem(i - kept, ring)
-        copy(i, slot).wait()
-        add(i, buf[slot])
-
-        @pl.when(i + ring < pieces)
-        def _():
-            copy(i + ring, slot).start()
-
-        return carry
-
-    lax.fori_loop(0, kept, early, 0)
-    if pieces > kept:
-        lax.fori_loop(kept, pieces, piece, 0)
+    units = 2 if tn % (2 * UNIT) == 0 else 1
+    height = groups * rows
+    sets = 2 if 2 * height <= SUM_ROWS else 1
+
+    def work(*flat):
+        sums = [flat[u * sets : (u + 1) * sets] for u in range(units)]
+
+        def tile(t, carry):
+            piece = (first_tile + t) * members
+            for m in range(members):
+
+                @pl.when(piece + m >= have)
+                def _():
+                    copy(piece + m).wait()
+
+            add(t, lax.rem(piece, slots), sums)
+            for m in range(members):
+
+                @pl.when(jnp.logical_and(piece + m + slots >= have, piece + m + slots < want))
+                def _():
+                    copy(piece + m + slots).start()
+
+            return carry
+
+        lax.fori_loop(0, tiles, tile, 0)
+
+    pl.run_scoped(work, *[pltpu.ACC(mxu_id=u)((height, UNIT), jnp.float32) for u in range(units) for _ in range(sets)])
     own_ref[...] = acc[:rows, :]
     for k in range(1, groups):
-        encode(acc[k * rows : (k + 1) * rows, :], msg_refs[k - 1])
-
-
-def chunk(blocks, factor, kept, screened, start, width, tn, after):
+        encode(acc[k * rows : (k + 1) * rows, :], msg_refs[order(groups).index(k)])
+    for i in range(max(have, end), want):
+        copy(i).wait()
+
+
+def chunk(blocks, factor, ring, screened, first_tile, width, have, want, tn):
     groups, (rows, depth) = len(blocks), blocks[0].shape
     members = screened.shape[0]
-    ring = 4
     outs = [jax.ShapeDtypeStruct((rows, width), jnp.float32)]
     outs += [jax.ShapeDtypeStruct((rows, width + LANES), jnp.int16)] * (groups - 1)
+    outs += [pltpu.VMEM(ring.shape, ring.dtype)]
     return pl.pallas_call(
-        functools.partial(chunk_kernel, groups, start, tn, ring, len(after)),
-        in_specs=[VMEM] * (groups + 2) + [ANY] * (1 + len(after)),
-        out_specs=[VMEM] * groups,
+        functools.partial(chunk_kernel, groups, first_tile, have, want, tn),
+        in_specs=[VMEM] * (groups + 1) + [HBM, VMEM],
+        out_specs=[VMEM] * (groups + 1),
         out_shape=outs,
+        input_output_aliases={groups + 2: groups},
         scratch_shapes=[
             pltpu.VMEM((groups * rows, depth), jnp.bfloat16),
             pltpu.VMEM((groups * rows, width), jnp.float32),
-            pltpu.VMEM((ring, depth, tn), jnp.bfloat16),
-            pltpu.SemaphoreType.DMA((ring,)),
+            pltpu.SemaphoreType.DMA((ring.shape[0],)),
         ],
-        compiler_params=pltpu.CompilerParams(vmem_limit_bytes=20 << 20),
+        compiler_params=pltpu.CompilerParams(vmem_limit_bytes=8 << 20),
         cost_estimate=pl.CostEstimate(
             flops=2 * groups * rows * depth * width * members,
             bytes_accessed=2 * members * depth * width,
             transcendentals=0,
         ),
         name="weighted_products",
-    )(*blocks, factor, kept, screened, *after)
+    )(*blocks, factor, screened, ring)
 
 
 def middle_kernel(groups, members, widths, after, *refs):
@@ -269,8 +314,8 @@
                 picked[k] = total[target * each : (target + 1) * each, :]
 
     mine_ref[...] = picked[0]
-    for k in range(1, members):
-        fold(picked[k], out_refs[k - 1], work)
+    for k, out_ref in zip(order(members), out_refs):
+        fold(picked[k], out_ref, work)
 
 
 def middle(chunks, members, after):
@@ -333,20 +378,24 @@
     tn = math.gcd(columns, 512)
     blocks = [pair_block] + [fetch(pair_block, "freq", k, groups) for k in range(1, groups)]
     widths = split(columns, tn)
-    starts = [sum(widths[:c]) for c in range(len(widths))]
-    plan = [(start, min(KEPT, width // tn * slots)) for start, width in zip(starts, widths)]
     smalls = (pair_gaps, omega_values, quad_weight, freq_slot, block_list)
-    factor, *kept = ahead(screened, smalls, groups * pair_block.shape[0], plan, tn)
-    made, after = [], []
-    for c, width in enumerate(widths):
-        made.append(chunk(blocks, factor, kept[c], screened, starts[c], width, tn, after))
-        after = [made[-1][0]]
-    sums = [[own] + [send(m, "freq", k + 1, groups) for k, m in enumerate(out)] for own, *out in made]
+    total = columns // tn * slots
+    have = min(EARLY * slots, total)
+    factor, ring = ahead(screened, smalls, groups * pair_block.shape[0], have, SPACE * slots, tn)
+    made, tile = [], 0
+    for width in widths:
+        first, tile = tile, tile + width // tn
+        want = min((tile + NEXT) * slots, total)
+        *out, ring = chunk(blocks, factor, ring, screened, first, width, have, want, tn)
+        have = want
+        made.append(out)
+    after = [made[-1][0]]
+    sums = [[own] + send_all(out, "freq", groups) for own, *out in made]
     parts, lasts = [], []
     for some in (sums[:-1], sums[-1:]):
         if some:
             mine, *out = middle(some, members, after)
-            parts += [mine] + [send(m, "row", k + 1, members) for k, m in enumerate(out)]
+            parts += [mine] + send_all(out, "row", members)
             lasts.append(mine.shape[1])
             after = parts[-members + 1 :][:DEPENDS]
     return last(parts, lasts, members)

time: 59.9 us -> 56.4 us (0.942)
  Pallas kernels: 30.6 us -> 28.1 us
  starting transfers between devices: 22.2 us -> 21.6 us
    pallas_call x3, Pallas kernels: 28.3 us -> 25.9 us  [the longest x2 17.3 us: chunk(): pl.pallas_call(functools.partial(chunk_kernel, groups, first_tile, have,...]
    ppermute x3, waiting for transfers between devices: 1.65 us -> 0.33 us  [fetch(): return lax.ppermute(array, axis, [(peer(i, k, n), i) for i in range(n)])]
    ppermute x12, waiting for transfers between devices: 5.29 us -> 6.27 us  [send(): return lax.ppermute(array, axis, [(i, peer(i, k, n)) for i in range(n)])]
    ppermute x12, starting transfers between devices: 17.7 us -> 17 us  [send(): return lax.ppermute(array, axis, [(i, peer(i, k, n)) for i in range(n)])]
  transfers between devices with their start and end apart: 15 -> 15, of which waited for: 6 -> 7; matrix products, arithmetic and copies ran while one was open for 0% -> 0% of each run, Pallas kernels for 28% -> 33%
where the time goes in v3:
time: 56.4 us; the launch traced here: 56.3 us
  Pallas kernels  28.1 us (50%)
  starting transfers between devices  21.6 us (38%)
  waiting for transfers between devices  6.6 us (12%)
    pallas_call x2, Pallas kernels, chunk(): pl.pallas_call(functools.partial(chunk_kernel, groups, first_tile, have,...  17.3 us
    ppermute x12, starting transfers between devices, send(): return lax.ppermute(array, axis, [(i, peer(i, k, n)) for i in range(n)])  17 us
    pallas_call x1, Pallas kernels, ahead(): pl.pallas_call(functools.partial(ahead_kernel, count, tn), in_specs=[HBM]...  8.64 us
    ppermute x12, waiting for transfers between devices, send(): return lax.ppermute(array, axis, [(i, peer(i, k, n)) for i in range(n)])  6.27 us
    ppermute x3, starting transfers between devices, fetch(): return lax.ppermute(array, axis, [(peer(i, k, n), i) for i in range(n)])  4.52 us
    pallas_call x2, Pallas kernels, middle(): pl.pallas_call(functools.partial(middle_kernel, len(chunks[0]), members,...  1.26 us
  transfers between devices with their start and end apart: 15, of which 7 were waited for; matrix products, arithmetic and copies ran while one was open for 0% of the time, Pallas kernels for 33%

profile of v3, /device:TPU:0, one launch (start us, length us, event | category | flops | bytes accessed | tf_op | source)
XLA Modules:
  0.0 56.3 jit_solution(9877472849793606998)
XLA Ops:
  0.0 0.0 copy-start
  0.0 3.9 %collective-permute-start.2 = (bf16[48,2048]{1,0:T(8,128)(2,1)}, bf16[48,2048]{1,0:T(8,128)(2,1)S(1)}, u32[]{:S(2)}, u32[]{:S(2)}) collective-permute-start(bf16[48,2048]{1,0:T(8,128)(2,1)} %refs_0_.5), channel_id=1, source_target_pairs={{24,0},{16,8},{8,16},{0,24},{25,1},{17,9},{9,17},{1,25},{26,2},{18... | collective-permute-start | bytes 589832 | tf_op jit(solution)/shard_map/ppermute | solution.py:41
  3.9 0.5 collective-permute-start.1
  4.4 0.1 collective-permute-start
  4.5 8.6 %pieces_ahead.1 = (f32[4,192,128]{2,1,0:T(8,128)S(1)}, bf16[20,2048,512]{2,1,0:T(8,128)(2,1)S(1)}) custom-call(bf16[4,2048,4096]{2,1,0:T(8,128)(2,1)} %refs_5_.3, f32[192]{0:T(256)} %refs_0_.3, f32[16]{0:T(128)} %refs_1_.1, f32[16]{0:T(128)} %refs_2_.1, s32[16]{0:T(128)} %refs_3_.1, s32[16]{0:T(128)} %refs_4_.1), custom_call_target="tpu_custom_call" | custom-call | bytes 25165824 | tf_op jit(solution)/shard_map/pieces_ahead/pallas_call | solution.py:161
  13.2 0.0 collective-permute-done.2.refs_3_
  13.2 0.1 collective-permute-done.1.refs_2_
  13.3 0.2 collective-permute-done.refs_1_
  13.5 0.0 copy-done
  13.5 8.8 %weighted_products.2 = (f32[48,2048]{1,0:T(8,128)S(1)}, s16[48,2176]{1,0:T(8,128)(2,1)S(1)}, s16[48,2176]{1,0:T(8,128)(2,1)S(1)}, s16[48,2176]{1,0:T(8,128)(2,1)S(1)}, bf16[20,2048,512]{2,1,0:T(8,128)(2,1)S(1)}) custom-call(bf16[48,2048]{1,0:T(8,128)(2,1)S(1)} %copy-done, ...), custom_call_target="tpu_custom_call", output_to_operand_aliasing={{4}: (6, {})} | custom-call | flops 6442450944 | bytes 33554432 | tf_op jit(solution)/shard_map/weighted_products/pallas_call | solution.py:274
  22.4 2.6 %collective-permute-start.3 = (s16[48,2176]{1,0:T(8,128)(2,1)S(1)}, s16[48,2176]{1,0:T(8,128)(2,1)S(1)}, u32[]{:S(2)}, u32[]{:S(2)}) collective-permute-start(s16[48,2176]{1,0:T(8,128)(2,1)S(1)} %get-tuple-element.27), channel_id=1, source_target_pairs={{0,24},{8,16},{16,8},{24,0},{1,25},{9,17},{17,9},{25,1},{2,26},{10... | collective-permute-start | bytes 626696 | tf_op jit(solution)/shard_map/ppermute | solution.py:29
  25.0 0.5 collective-permute-start.4
  25.5 0.4 collective-permute-start.5
  25.9 8.4 %weighted_products.3 = (f32[48,2048]{1,0:T(8,128)S(1)}, s16[48,2176]{1,0:T(8,128)(2,1)S(1)}, s16[48,2176]{1,0:T(8,128)(2,1)S(1)}, s16[48,2176]{1,0:T(8,128)(2,1)S(1)}, bf16[20,2048,512]{2,1,0:T(8,128)(2,1)S(1)}) custom-call(bf16[48,2048]{1,0:T(8,128)(2,1)S(1)} %copy-done, ...), custom_call_target="tpu_custom_call", output_to_operand_aliasing={{4}: (6, {})} | custom-call | flops 6442450944 | bytes 33554432 | tf_op jit(solution)/shard_map/weighted_products/pallas_call | solution.py:274
  34.3 2.6 %collective-permute-start.9 = (s16[48,2176]{1,0:T(8,128)(2,1)S(1)}, s16[48,2176]{1,0:T(8,128)(2,1)S(1)}, u32[]{:S(2)}, u32[]{:S(2)}) collective-permute-start(s16[48,2176]{1,0:T(8,128)(2,1)S(1)} %get-tuple-element.36), channel_id=1, source_target_pairs={{0,24},{8,16},{16,8},{24,0},{1,25},{9,17},{17,9},{25,1},{2,26},{10... | collective-permute-start | bytes 626696 | tf_op jit(solution)/shard_map/ppermute | solution.py:29
  37.0 0.5 collective-permute-start.10
  37.5 0.0 collective-permute-done.3.refs_1_
  37.5 0.4 collective-permute-start.11
  37.9 0.0 collective-permute-done.4.refs_2_
  37.9 0.0 collective-permute-done.5.refs_3_
  37.9 0.6 %frequency_sums.2 = (f32[12,2048]{1,0:T(8,128)S(1)}, s16[16,1664]{1,0:T(8,128)(2,1)S(1)}, s16[16,1664]{1,0:T(8,128)(2,1)S(1)}, s16[16,1664]{1,0:T(8,128)(2,1)S(1)}) custom-call(f32[48,2048]{1,0:T(8,128)S(1)} %get-tuple-element.26.refs_0_, s16[48,2176]{1,0:T(8,128)(2,1)S(1)} %collective-permute-done.3.refs_1_, ...), custom_call_target="tpu_custom_call" | custom-call | tf_op jit(solution)/shard_map/frequency_sums/pallas_call | solution.py:329
  38.5 3.8 %collective-permute-start.6 = (s16[16,1664]{1,0:T(8,128)(2,1)S(1)}, s16[16,1664]{1,0:T(8,128)(2,1)S(1)}, u32[]{:S(2)}, u32[]{:S(2)}) collective-permute-start(s16[16,1664]{1,0:T(8,128)(2,1)S(1)} %get-tuple-element.33), channel_id=1, source_target_pairs={{0,6},{2,4},{4,2},{6,0},{1,7},{3,5},{5,3},{7,1},{8,14},{10,12},{12... | collective-permute-start | bytes 159752 | tf_op jit(solution)/shard_map/ppermute | solution.py:29
  42.3 0.0 collective-permute-start.7
  42.3 1.1 %collective-permute-done.9.refs_1_ = s16[48,2176]{1,0:T(8,128)(2,1)S(1)} collective-permute-done((s16[48,2176]{1,0:T(8,128)(2,1)S(1)}, s16[48,2176]{1,0:T(8,128)(2,1)S(1)}, u32[]{:S(2)}, u32[]{:S(2)}) %collective-permute-start.9) | collective-permute-done | bytes 208928 | tf_op jit(solution)/shard_map/ppermute | solution.py:29
  43.4 1.7 %collective-permute-start.8 = (s16[16,1664]{1,0:T(8,128)(2,1)S(1)}, s16[16,1664]{1,0:T(8,128)(2,1)S(1)}, u32[]{:S(2)}, u32[]{:S(2)}) collective-permute-start(s16[16,1664]{1,0:T(8,128)(2,1)S(1)} %get-tuple-element.35), channel_id=1, source_target_pairs={{0,2},{2,0},{4,6},{6,4},{1,3},{3,1},{5,7},{7,5},{8,10},{10,8},{12,... | collective-permute-start | bytes 159752 | tf_op jit(solution)/shard_map/ppermute | solution.py:29
  45.1 0.7 %collective-permute-done.10.refs_2_ = s16[48,2176]{1,0:T(8,128)(2,1)S(1)} collective-permute-done((s16[48,2176]{1,0:T(8,128)(2,1)S(1)}, s16[48,2176]{1,0:T(8,128)(2,1)S(1)}, u32[]{:S(2)}, u32[]{:S(2)}) %collective-permute-start.10) | collective-permute-done | bytes 208928 | tf_op jit(solution)/shard_map/ppermute | solution.py:29
  45.8 0.2 collective-permute-done.11.refs_3_
  46.0 0.0 collective-permute-done.6.refs_4_.refs_1_
  46.0 0.6 %frequency_sums.3 = (f32[12,2048]{1,0:T(8,128)S(1)}, s16[16,1664]{1,0:T(8,128)(2,1)S(1)}, s16[16,1664]{1,0:T(8,128)(2,1)S(1)}, s16[16,1664]{1,0:T(8,128)(2,1)S(1)}) custom-call(f32[48,2048]{1,0:T(8,128)S(1)} %get-tuple-element.31.refs_4_.refs_0_, s16[48,2176]{1,0:T(8,128)(2,1)S(1)} %collective-permute-done.9.refs_1_, ...), custom_call_target="tpu_custom_call" | custom-call | tf_op jit(solution)/shard_map/frequency_sums/pallas_call | solution.py:329
  46.7 3.7 %collective-permute-start.12 = (s16[16,1664]{1,0:T(8,128)(2,1)S(1)}, s16[16,1664]{1,0:T(8,128)(2,1)S(1)}, u32[]{:S(2)}, u32[]{:S(2)}) collective-permute-start(s16[16,1664]{1,0:T(8,128)(2,1)S(1)} %get-tuple-element.40), channel_id=1, source_target_pairs={{0,6},{2,4},{4,2},{6,0},{1,7},{3,5},{5,3},{7,1},{8,14},{10,12},{12... | collective-permute-start | bytes 159752 | tf_op jit(solution)/shard_map/ppermute | solution.py:29
  50.3 0.0 collective-permute-start.13
  50.3 0.8 %collective-permute-start.14 = (s16[16,1664]{1,0:T(8,128)(2,1)S(1)}, s16[16,1664]{1,0:T(8,128)(2,1)S(1)}, u32[]{:S(2)}, u32[]{:S(2)}) collective-permute-start(s16[16,1664]{1,0:T(8,128)(2,1)S(1)} %get-tuple-element.42), channel_id=1, source_target_pairs={{0,2},{2,0},{4,6},{6,4},{1,3},{3,1},{5,7},{7,5},{8,10},{10,8},{12,... | collective-permute-start | bytes 159752 | tf_op jit(solution)/shard_map/ppermute | solution.py:29
  51.1 0.0 collective-permute-done.7.refs_2_
  51.1 0.0 collective-permute-done.8.refs_3_
  51.1 2.0 %collective-permute-done.12.refs_5_ = s16[16,1664]{1,0:T(8,128)(2,1)S(1)} collective-permute-done((s16[16,1664]{1,0:T(8,128)(2,1)S(1)}, s16[16,1664]{1,0:T(8,128)(2,1)S(1)}, u32[]{:S(2)}, u32[]{:S(2)}) %collective-permute-start.12) | collective-permute-done | bytes 53280 | tf_op jit(solution)/shard_map/ppermute | solution.py:29
  53.1 2.2 %collective-permute-done.13.refs_6_ = s16[16,1664]{1,0:T(8,128)(2,1)S(1)} collective-permute-done((s16[16,1664]{1,0:T(8,128)(2,1)S(1)}, s16[16,1664]{1,0:T(8,128)(2,1)S(1)}, u32[]{:S(2)}, u32[]{:S(2)}) %collective-permute-start.13) | collective-permute-done | bytes 53280 | tf_op jit(solution)/shard_map/ppermute | solution.py:29
  55.4 0.0 collective-permute-done.14.refs_7_
  55.4 0.9 %row_sums.1 = f32[12,4096]{1,0:T(8,128)} custom-call(f32[12,2048]{1,0:T(8,128)S(1)} %get-tuple-element.32.refs_0_, s16[16,1664]{1,0:T(8,128)(2,1)S(1)} %collective-permute-done.6.refs_4_.refs_1_, s16[16,1664]{1,0:T(8,128)(2,1)S(1)} %collective-permute-done.7.refs_2_, s16[16,1664]{1,0:T(8,128)(2,1)S(1)} %collective-permute-done.8.refs_3_, ...), custom_call_target="tpu_custom_call" | custom-call | tf_op jit(solution)/shard_map/row_sums/pallas_call | solution.py:358
Async XLA Ops:
  0.0 13.5 %copy-start = (bf16[48,2048]{1,0:T(8,128)(2,1)S(1)}, bf16[48,2048]{1,0:T(8,128)(2,1)}, u32[]{:S(2)}) copy-start(bf16[48,2048]{1,0:T(8,128)(2,1)} %refs_0_.5) | copy-start | bytes 589828
  0.0 13.2 %collective-permute-start.2 = (bf16[48,2048]{1,0:T(8,128)(2,1)}, bf16[48,2048]{1,0:T(8,128)(2,1)S(1)}, u32[]{:S(2)}, u32[]{:S(2)}) collective-permute-start(bf16[48,2048]{1,0:T(8,128)(2,1)} %refs_0_.5), channel_id=1, source_target_pairs={{24,0},{16,8},{8,16},{0,24},{25,1},{17,9},{9,17},{1,25},{26,2},{18... | collective-permute-start | bytes 589832 | tf_op jit(solution)/shard_map/ppermute | solution.py:41
  3.9 9.4 %collective-permute-start.1 = (bf16[48,2048]{1,0:T(8,128)(2,1)}, bf16[48,2048]{1,0:T(8,128)(2,1)S(1)}, u32[]{:S(2)}, u32[]{:S(2)}) collective-permute-start(bf16[48,2048]{1,0:T(8,128)(2,1)} %refs_0_.5), channel_id=1, source_target_pairs={{16,0},{24,8},{0,16},{8,24},{17,1},{25,9},{1,17},{9,25},{18,2},{26... | collective-permute-start | bytes 589832 | tf_op jit(solution)/shard_map/ppermute | solution.py:41
  4.4 9.1 %collective-permute-start = (bf16[48,2048]{1,0:T(8,128)(2,1)}, bf16[48,2048]{1,0:T(8,128)(2,1)S(1)}, u32[]{:S(2)}, u32[]{:S(2)}) collective-permute-start(bf16[48,2048]{1,0:T(8,128)(2,1)} %refs_0_.5), channel_id=1, source_target_pairs={{8,0},{0,8},{24,16},{16,24},{9,1},{1,9},{25,17},{17,25},{10,2},{2,... | collective-permute-start | bytes 589832 | tf_op jit(solution)/shard_map/ppermute | solution.py:41
  22.4 15.1 %collective-permute-start.3 = (s16[48,2176]{1,0:T(8,128)(2,1)S(1)}, s16[48,2176]{1,0:T(8,128)(2,1)S(1)}, u32[]{:S(2)}, u32[]{:S(2)}) collective-permute-start(s16[48,2176]{1,0:T(8,128)(2,1)S(1)} %get-tuple-element.27), channel_id=1, source_target_pairs={{0,24},{8,16},{16,8},{24,0},{1,25},{9,17},{17,9},{25,1},{2,26},{10... | collective-permute-start | bytes 626696 | tf_op jit(solution)/shard_map/ppermute | solution.py:29
  25.0 12.9 %collective-permute-start.4 = (s16[48,2176]{1,0:T(8,128)(2,1)S(1)}, s16[48,2176]{1,0:T(8,128)(2,1)S(1)}, u32[]{:S(2)}, u32[]{:S(2)}) collective-permute-start(s16[48,2176]{1,0:T(8,128)(2,1)S(1)} %get-tuple-element.28), channel_id=1, source_target_pairs={{0,16},{8,24},{16,0},{24,8},{1,17},{9,25},{17,1},{25,9},{2,18},{10... | collective-permute-start | bytes 626696 | tf_op jit(solution)/shard_map/ppermute | solution.py:29
  25.5 12.4 %collective-permute-start.5 = (s16[48,2176]{1,0:T(8,128)(2,1)S(1)}, s16[48,2176]{1,0:T(8,128)(2,1)S(1)}, u32[]{:S(2)}, u32[]{:S(2)}) collective-permute-start(s16[48,2176]{1,0:T(8,128)(2,1)S(1)} %get-tuple-element.29), channel_id=1, source_target_pairs={{0,8},{8,0},{16,24},{24,16},{1,9},{9,1},{17,25},{25,17},{2,10},{10... | collective-permute-start | bytes 626696 | tf_op jit(solution)/shard_map/ppermute | solution.py:29
  34.3 9.1 %collective-permute-start.9 = (s16[48,2176]{1,0:T(8,128)(2,1)S(1)}, s16[48,2176]{1,0:T(8,128)(2,1)S(1)}, u32[]{:S(2)}, u32[]{:S(2)}) collective-permute-start(s16[48,2176]{1,0:T(8,128)(2,1)S(1)} %get-tuple-element.36), channel_id=1, source_target_pairs={{0,24},{8,16},{16,8},{24,0},{1,25},{9,17},{17,9},{25,1},{2,26},{10... | collective-permute-start | bytes 626696 | tf_op jit(solution)/shard_map/ppermute | solution.py:29
  37.0 8.8 %collective-permute-start.10 = (s16[48,2176]{1,0:T(8,128)(2,1)S(1)}, s16[48,2176]{1,0:T(8,128)(2,1)S(1)}, u32[]{:S(2)}, u32[]{:S(2)}) collective-permute-start(s16[48,2176]{1,0:T(8,128)(2,1)S(1)} %get-tuple-element.37), channel_id=1, source_target_pairs={{0,16},{8,24},{16,0},{24,8},{1,17},{9,25},{17,1},{25,9},{2,18},{10... | collective-permute-start | bytes 626696 | tf_op jit(solution)/shard_map/ppermute | solution.py:29
  37.5 8.6 %collective-permute-start.11 = (s16[48,2176]{1,0:T(8,128)(2,1)S(1)}, s16[48,2176]{1,0:T(8,128)(2,1)S(1)}, u32[]{:S(2)}, u32[]{:S(2)}) collective-permute-start(s16[48,2176]{1,0:T(8,128)(2,1)S(1)} %get-tuple-element.38), channel_id=1, source_target_pairs={{0,8},{8,0},{16,24},{24,16},{1,9},{9,1},{17,25},{25,17},{2,10},{10... | collective-permute-start | bytes 626696 | tf_op jit(solution)/shard_map/ppermute | solution.py:29
  38.5 7.5 %collective-permute-start.6 = (s16[16,1664]{1,0:T(8,128)(2,1)S(1)}, s16[16,1664]{1,0:T(8,128)(2,1)S(1)}, u32[]{:S(2)}, u32[]{:S(2)}) collective-permute-start(s16[16,1664]{1,0:T(8,128)(2,1)S(1)} %get-tuple-element.33), channel_id=1, source_target_pairs={{0,6},{2,4},{4,2},{6,0},{1,7},{3,5},{5,3},{7,1},{8,14},{10,12},{12... | collective-permute-start | bytes 159752 | tf_op jit(solution)/shard_map/ppermute | solution.py:29
  42.3 8.8 %collective-permute-start.7 = (s16[16,1664]{1,0:T(8,128)(2,1)S(1)}, s16[16,1664]{1,0:T(8,128)(2,1)S(1)}, u32[]{:S(2)}, u32[]{:S(2)}) collective-permute-start(s16[16,1664]{1,0:T(8,128)(2,1)S(1)} %get-tuple-element.34), channel_id=1, source_target_pairs={{0,4},{2,6},{4,0},{6,2},{1,5},{3,7},{5,1},{7,3},{8,12},{10,14},{12... | collective-permute-start | bytes 159752 | tf_op jit(solution)/shard_map/ppermute | solution.py:29
  43.4 7.7 %collective-permute-start.8 = (s16[16,1664]{1,0:T(8,128)(2,1)S(1)}, s16[16,1664]{1,0:T(8,128)(2,1)S(1)}, u32[]{:S(2)}, u32[]{:S(2)}) collective-permute-start(s16[16,1664]{1,0:T(8,128)(2,1)S(1)} %get-tuple-element.35), channel_id=1, source_target_pairs={{0,2},{2,0},{4,6},{6,4},{1,3},{3,1},{5,7},{7,5},{8,10},{10,8},{12,... | collective-permute-start | bytes 159752 | tf_op jit(solution)/shard_map/ppermute | solution.py:29
  46.7 6.5 %collective-permute-start.12 = (s16[16,1664]{1,0:T(8,128)(2,1)S(1)}, s16[16,1664]{1,0:T(8,128)(2,1)S(1)}, u32[]{:S(2)}, u32[]{:S(2)}) collective-permute-start(s16[16,1664]{1,0:T(8,128)(2,1)S(1)} %get-tuple-element.40), channel_id=1, source_target_pairs={{0,6},{2,4},{4,2},{6,0},{1,7},{3,5},{5,3},{7,1},{8,14},{10,12},{12... | collective-permute-start | bytes 159752 | tf_op jit(solution)/shard_map/ppermute | solution.py:29
  50.3 5.0 %collective-permute-start.13 = (s16[16,1664]{1,0:T(8,128)(2,1)S(1)}, s16[16,1664]{1,0:T(8,128)(2,1)S(1)}, u32[]{:S(2)}, u32[]{:S(2)}) collective-permute-start(s16[16,1664]{1,0:T(8,128)(2,1)S(1)} %get-tuple-element.41), channel_id=1, source_target_pairs={{0,4},{2,6},{4,0},{6,2},{1,5},{3,7},{5,1},{7,3},{8,12},{10,14},{12... | collective-permute-start | bytes 159752 | tf_op jit(solution)/shard_map/ppermute | solution.py:29
  50.3 5.0 %collective-permute-start.14 = (s16[16,1664]{1,0:T(8,128)(2,1)S(1)}, s16[16,1664]{1,0:T(8,128)(2,1)S(1)}, u32[]{:S(2)}, u32[]{:S(2)}) collective-permute-start(s16[16,1664]{1,0:T(8,128)(2,1)S(1)} %get-tuple-element.42), channel_id=1, source_target_pairs={{0,2},{2,0},{4,6},{6,4},{1,3},{3,1},{5,7},{7,5},{8,10},{10,8},{12,... | collective-permute-start | bytes 159752 | tf_op jit(solution)/shard_map/ppermute | solution.py:29
